TPU v7x, 512 devices: a whole 4x4x16 slice. The times are simulated.
512 devices in a mesh: dp: 64 (over z, x), col: 8 (over y, core).
Axes of the slice: x: 4, y: 4, z: 16, core: 2. Of those that a mesh axis runs over, the one named last changes fastest.
Arguments:
- jacobian: bfloat16 [131072, 4096], P('dp', 'col'), may hold values from -6 to 6
- residual: float32 [131072], P('dp'), may hold values from -6 to 6
- bucket: int32 [131072], P('dp'), may hold values from 0 to 767
- sign_bit: int32 [131072], P('dp'), may hold values from 0 to 1
Outputs:
- update: float32 [4096], P('col')
- sketched: float32 [768, 4096], P('dp', 'col')
All inputs are finite; a program needn't handle non-finite values.
Results may differ from a plain program's by a relative error of at most 0.0003.
Values sent between devices are 32-bit elements; how exact they have to be, the bound alone decides.
A program may use at most 64 MiB of HBM per device.

v0:
```python
import math

import jax
import jax.numpy as jnp
from jax import lax
from jax.sharding import PartitionSpec as P

PARAMS = 4096
SK_DEV = 12


def on_device(jacobian, residual, bucket, sign_bit):
    row_count, col_count = jacobian.shape
    dp_count = lax.axis_size("dp")
    sketch_rows = SK_DEV * dp_count
    scaling = math.sqrt(sketch_rows / (row_count * dp_count))
    sign_values = (2 * sign_bit - 1).astype(jnp.bfloat16)
    block_rows = min(512, row_count)
    block_count = row_count // block_rows
    targets = jnp.arange(sketch_rows, dtype=jnp.int32)[:, None]

    def add_block(block_index, carry):
        first = block_index * block_rows
        jac_piece = lax.dynamic_slice_in_dim(jacobian, first, block_rows, 0)
        res_piece = lax.dynamic_slice_in_dim(residual, first, block_rows, 0)
        buck_piece = lax.dynamic_slice_in_dim(bucket, first, block_rows, 0)
        sign_piece = lax.dynamic_slice_in_dim(sign_values, first, block_rows, 0)
        onehot = jnp.where(
            buck_piece[None, :] == targets, sign_piece[None, :], jnp.zeros((), jnp.bfloat16)
        )
        total_jac = carry[0] + jnp.dot(onehot, jac_piece, preferred_element_type=jnp.float32)
        total_res = carry[1] + jnp.dot(
            onehot.astype(jnp.float32), res_piece, precision=lax.Precision.HIGHEST
        )
        return (total_jac, total_res)

    start = (
        jnp.zeros((sketch_rows, col_count), jnp.float32),
        jnp.zeros((sketch_rows,), jnp.float32),
    )
    partial_jac, partial_res = lax.fori_loop(0, block_count, add_block, start)
    whole_jac, whole_res = lax.psum((partial_jac, partial_res), "dp")
    sketched = whole_jac * scaling
    rhs = whole_res * scaling
    owned = lax.dynamic_slice_in_dim(sketched, lax.axis_index("dp") * SK_DEV, SK_DEV, 0)
    partial_rows = jnp.dot(owned, sketched.T, precision=lax.Precision.HIGHEST)
    summed_rows = lax.psum(partial_rows, "col")
    kernel = lax.all_gather(summed_rows, "dp", axis=0, tiled=True) / PARAMS
    kernel = kernel + 0.5 * jnp.eye(sketch_rows, dtype=jnp.float32)
    factor = jnp.linalg.cholesky(kernel)
    middle = lax.linalg.triangular_solve(factor, rhs[:, None], left_side=True, lower=True)
    dual_vec = lax.linalg.triangular_solve(
        factor, middle, left_side=True, lower=True, transpose_a=True
    )
    update = jnp.dot(sketched.T, dual_vec[:, 0], precision=lax.Precision.HIGHEST) / math.sqrt(
        PARAMS
    )
    return (update, owned)


def solution(mesh):
    return jax.shard_map(
        on_device,
        mesh=mesh,
        in_specs=(P("dp", "col"), P("dp"), P("dp"), P("dp")),
        out_specs=(P("col"), P("dp", "col")),
        check_vma=False,
    )
```

profile of v0, /device:TPU:1, one launch (start us, length us, event | category | flops | bytes accessed | tf_op | source)
XLA Modules:
  0.0 716.8 jit_solution(14289250080433264286)
XLA Ops:
  7.9 16.6 %while.18 = (s32[]{:T(128)}, f32[768,512]{1,0:T(8,128)S(1)}, f32[768]{0:T(1024)S(1)}, s32[2048]{0:T(1024)}, bf16[2048]{0:T(1024)(128)(2,1)S(1)}, /*index=5*/bf16...) while((s32[]{:T(128)}, f32[768,512]{1,0:T(8,128)S(1)}, ...), condition=%wide.region_1.2_spmd.clone, body=%wide.region_0.1_spmd.clone.sunk | while | flops 409732608 | bytes 3700918 | solution.py:41
  8.8 1.8 select_add_fusion.5
  12.9 1.8 select_add_fusion.5
  17.1 1.8 select_add_fusion.5
  21.3 1.8 select_add_fusion.5
  25.8 272.9 %all-reduce.3.cloned.1.call-done = f32[768,512]{1,0:T(8,128)} async-done(((f32[768,512]{1,0:T(8,128)}), f32[768,512]{1,0:T(8,128)}) %all-reduce.3.cloned.1.call-update) | async-done | bytes 1572880 | tf_op jit(solution)/shard_map/psum | solution.py:42
  298.7 1.7 broadcast_multiply_fusion.1
  300.6 1.3 fusion.112
  301.9 31.3 %psum.22 = f32[12,768]{1,0:T(8,128)} all-reduce(f32[12,768]{1,0:T(8,128)S(1)} %fusion.112), channel_id=1, replica_groups=mesh['dp'=64,'col'=8] {'col'}, use_global_device_ids=true, to_apply=%region_3.4 | all-reduce | flops 9216 | bytes 73728 | tf_op jit(solution)/shard_map/psum | solution.py:47
  333.3 113.1 %psum.23 = f32[768]{0:T(1024)S(1)} all-reduce(f32[768]{0:T(1024)S(1)} %get-tuple-element.143), channel_id=1, replica_groups=mesh['dp'=64,'col'=8] {'dp'}, use_global_device_ids=true, to_apply=%region_16.17 | all-reduce | flops 768 | bytes 6144 | tf_op jit(solution)/shard_map/psum | solution.py:42
  446.4 18.0 %all-gather.3.cloned.1.call-done = f32[64,12,768]{2,1,0:T(8,128)} async-done(((f32[1,12,768]{2,1,0:T(8,128)}), f32[64,12,768]{2,1,0:T(8,128)}) %all-gather.3.cloned.1.call-update) | async-done | bytes 2359312 | tf_op jit(solution)/shard_map/all_gather | solution.py:48
  464.4 3.9 broadcast_multiply_fusion
  468.2 2.6 reshape.191
  470.9 1.6 select_add_fusion.2
  472.4 3.2 copy.8
  475.6 2.0 fusion.15
  477.6 1.4 copy-done.2
  479.0 11.7 %cholesky.164 = f32[128,128]{1,0:T(8,128)S(1)} custom-call(f32[128,128]{1,0:T(8,128)S(1)} %cholesky.421), custom_call_target="Cholesky" | custom-call | tf_op jit(solution)/shard_map/jit(cholesky)/cholesky | solution.py:50
  490.8 9.8 %custom-call.48 = f32[1,128,128]{1,2,0:T(8,128)S(1)} custom-call(f32[1,128,128]{2,1,0:T(8,128)S(1)} %get-tuple-element.217), custom_call_target="InvertDiagBlocksLowerTriangular" | custom-call | tf_op jit(solution)/shard_map/jit(cholesky)/cholesky | solution.py:50
  500.7 1.4 constant_dynamic-update-slice_fusion.20
  502.1 1.4 convolution_subtract_fusion
  503.5 11.7 %cholesky.187 = f32[128,128]{1,0:T(8,128)S(1)} custom-call(f32[128,128]{1,0:T(8,128)S(1)} %cholesky.425), custom_call_target="Cholesky" | custom-call | tf_op jit(solution)/shard_map/jit(cholesky)/cholesky | solution.py:50
  515.3 10.0 %custom-call.49 = f32[1,128,128]{1,2,0:T(8,128)S(1)} custom-call(f32[1,128,128]{2,1,0:T(8,128)S(1)} %get-tuple-element.214), custom_call_target="InvertDiagBlocksLowerTriangular" | custom-call | tf_op jit(solution)/shard_map/jit(cholesky)/cholesky | solution.py:50
  525.7 1.5 convolution_subtract_fusion.1
  527.2 11.7 %cholesky.352 = f32[128,128]{1,0:T(8,128)S(1)} custom-call(f32[128,128]{1,0:T(8,128)S(1)} %cholesky.430), custom_call_target="Cholesky" | custom-call | tf_op jit(solution)/shard_map/jit(cholesky)/cholesky | solution.py:50
  539.6 9.8 %custom-call.50 = f32[1,128,128]{1,2,0:T(8,128)S(1)} custom-call(f32[1,128,128]{2,1,0:T(8,128)S(1)} %get-tuple-element.211), custom_call_target="InvertDiagBlocksLowerTriangular" | custom-call | tf_op jit(solution)/shard_map/jit(cholesky)/cholesky | solution.py:50
  549.7 1.6 convolution_subtract_fusion.2
  551.3 12.1 %cholesky.371 = f32[128,128]{1,0:T(8,128)S(1)} custom-call(f32[128,128]{1,0:T(8,128)S(1)} %cholesky.435), custom_call_target="Cholesky" | custom-call | tf_op jit(solution)/shard_map/jit(cholesky)/cholesky | solution.py:50
  564.1 9.8 %custom-call.51 = f32[1,128,128]{1,2,0:T(8,128)S(1)} custom-call(f32[1,128,128]{2,1,0:T(8,128)S(1)} %get-tuple-element.208), custom_call_target="InvertDiagBlocksLowerTriangular" | custom-call | tf_op jit(solution)/shard_map/jit(cholesky)/cholesky | solution.py:50
  574.2 1.5 convolution_subtract_fusion.3
  575.7 11.7 %cholesky.390 = f32[128,128]{1,0:T(8,128)S(1)} custom-call(f32[128,128]{1,0:T(8,128)S(1)} %cholesky.440), custom_call_target="Cholesky" | custom-call | tf_op jit(solution)/shard_map/jit(cholesky)/cholesky | solution.py:50
  588.1 9.8 %custom-call.52 = f32[1,128,128]{1,2,0:T(8,128)S(1)} custom-call(f32[1,128,128]{2,1,0:T(8,128)S(1)} %get-tuple-element.205), custom_call_target="InvertDiagBlocksLowerTriangular" | custom-call | tf_op jit(solution)/shard_map/jit(cholesky)/cholesky | solution.py:50
  598.2 1.3 convolution_subtract_fusion.4
  599.5 11.9 %cholesky.408 = f32[128,128]{1,0:T(8,128)S(1)} custom-call(f32[128,128]{1,0:T(8,128)S(1)} %convolution_subtract_fusion.4), custom_call_target="Cholesky" | custom-call | tf_op jit(solution)/shard_map/jit(cholesky)/cholesky | solution.py:50
  616.5 1.6 select_select_fusion
  618.1 16.7 %while.17 = (s32[]{:T(128)}, f32[768,768]{1,0:T(8,128)}, s32[6,2]{0,1:T(2,128)S(1)}, f32[6,128,128]{2,1,0:T(8,128)S(1)}, s32[]{:T(128)}) while((s32[]{:T(128)}, f32[768,768]{1,0:T(8,128)}, s32[6,2]{0,1:T(2,128)S(1)}, f32[6,128,128]{2,1,0:T(8,128)S(1)}, s32[]{:T(128)}) %tuple.71), condition=%wide.while_cond, body=%wide.while_body.sunk | while | flops 2 | bytes 131181 | solution.py:52
  618.7 2.2 bitcast_dynamic-update-slice_fusion.2
  621.5 2.2 bitcast_dynamic-update-slice_fusion.2
  624.3 2.2 bitcast_dynamic-update-slice_fusion.2
  627.1 2.2 bitcast_dynamic-update-slice_fusion.2
  629.9 2.2 bitcast_dynamic-update-slice_fusion.2
  632.7 2.1 bitcast_dynamic-update-slice_fusion.2
  634.9 59.0 %custom-call.53 = f32[6,128,128]{1,2,0:T(8,128)S(1)} custom-call(f32[6,128,128]{2,1,0:T(8,128)S(1)} %get-tuple-element.151), custom_call_target="InvertDiagBlocksLowerTriangular" | custom-call | tf_op jit(solution)/shard_map/triangular_solve | solution.py:52
  696.5 1.2 fusion.38
  698.0 1.2 fusion.28
  699.4 1.4 fusion.36
  705.1 1.2 fusion.30
  706.6 1.3 fusion.32
  (102 shorter events, 29.6 us)
Async XLA Ops:
  7.2 291.5 %all-reduce.3.cloned.1.call-start = ((), (), s32[]{:S(2)}) async-start(), calls=%async_computation | async-start | bytes 3145728 | tf_op jit(solution)/shard_map/psum | solution.py:42
  24.6 1.2 copy-start.3
  25.8 438.6 %all-gather.3.cloned.1.call-start = ((), (), s32[]{:S(2)}) async-start(), calls=%async_computation.1 | async-start | bytes 3194880 | tf_op jit(solution)/shard_map/all_gather | solution.py:48
  298.7 1.9 copy-start
  300.6 167.7 %copy-start.4 = (f32[12,512]{1,0:T(8,128)}, f32[12,512]{1,0:T(8,128)S(1)}, u32[]{:S(2)}) copy-start(f32[12,512]{1,0:T(8,128)S(1)} %constant_dynamic-slice_fusion.1) | copy-start | bytes 73732
  477.6 1.4 copy-start.2
  618.1 90.1 %copy-start.1 = (f32[768,512]{1,0:T(8,128)S(1)}, f32[768,512]{1,0:T(8,128)}, u32[]{:S(2)}) copy-start(f32[768,512]{1,0:T(8,128)} %all-reduce.3.cloned.1.call-done) | copy-start | bytes 4718596
Sparse Core Ops, SparseCore 0:
  25.9 272.7 all-reduce.2
  333.4 130.9 all-gather.2
where the time goes:
time: 731 us; the launch traced here: 717 us
  waiting for transfers between devices  291 us (40%)
  other arithmetic  195 us (27%)
  blocking collectives  144 us (20%)
  matrix products  36.3 us (5%)
  local copies, waits for them, and re-layouts  31.9 us (4%)
  between operations  18.3 us (3%)
    psum x1, waiting for transfers between devices, on_device(): whole_jac, whole_res = lax.psum((partial_jac, partial_res), 'dp')  273 us
    another operation x22, other arithmetic, on_device(): factor = jnp.linalg.cholesky(kernel)  124 us
    psum x1, blocking collectives, on_device(): whole_jac, whole_res = lax.psum((partial_jac, partial_res), 'dp')  113 us
    another operation x3, other arithmetic, on_device(): lax.linalg.triangular_solve(factor, middle, left_side=True, lower=True, t...  60.5 us
    psum x1, blocking collectives, on_device(): summed_rows = lax.psum(partial_rows, 'col')  31.3 us
    all_gather x1, waiting for transfers between devices, on_device(): kernel = lax.all_gather(summed_rows, 'dp', axis=0, tiled=True) / PARAMS  18 us
    another operation x18, local copies, waits for them, and re-layouts  16.6 us
  transfers between devices with their start and end apart: 2, of which 2 were waited for; matrix products, arithmetic and copies ran while one was open for 0% of the time, Pallas kernels for 0%

commit v1 on v0

v1 whole, which is shorter than its diff:
```python
import functools
import math

import jax
import jax.numpy as jnp
from jax import lax
from jax.experimental import pallas as pl
from jax.experimental.pallas import tpu as pltpu
from jax.sharding import PartitionSpec as P

PARAMS = 4096
SKETCH = 768
DEV_ROWS = 2048
DEV_COLS = 512
LANES = 128
CHUNK = 48
GROUPS = DEV_ROWS // LANES
BLOCKS = SKETCH // LANES
TRI_ROWS = 2816
HALF = TRI_ROWS // 2
X_STRIP = HALF // 4
Y_STRIP = X_STRIP // 4
RHS_ROWS = 8
MESH = pl.DeviceIdType.MESH
HIGHEST = lax.Precision.HIGHEST
STOP_TOL = 3e-6
ACCEPT_TOL = 1e-5
ROUND_STEPS = 4
MAX_ROUNDS = 16


def place():
    dp, col = lax.axis_index("dp"), lax.axis_index("col")
    return dict(x=dp % 4, near=(dp // 4) % 4, far=dp // 16, y=col // 2, core=col % 2)


def peer(me, axis, step):
    at = dict(me)
    size = 2 if axis == "core" else 4
    at[axis] = (me[axis] + step) % size
    return (at["far"] * 16 + at["near"] * 4 + at["x"], at["y"] * 2 + at["core"])


def gather_kernel(
    scaling,
    jac_ref,
    res_ref,
    bucket_ref,
    sign_ref,
    tri_ref,
    rhs_ref,
    cols_ref,
    owned_ref,
    hot,
    acc,
    part,
    x_in,
    near_in,
    far_in,
    lhs,
    rhs_t,
    tri,
    core_in,
    kx_out,
    kx_in,
    ky_out,
    ky_in,
    send_sem,
    recv_sem,
):
    me = place()
    barrier = pltpu.get_barrier_semaphore()
    links = [(axis, step) for axis in ("x", "near", "far", "y") for step in (1, 2, 3)] + [("core", 1)]
    for axis, step in links:
        pl.semaphore_signal(barrier, inc=1, device_id=peer(me, axis, step), device_id_type=MESH)

    used = [0]

    def push(src, dst, axis, step):
        slot = used[0]
        used[0] += 1
        copy = pltpu.make_async_remote_copy(
            src_ref=src,
            dst_ref=dst,
            send_sem=send_sem.at[slot],
            recv_sem=recv_sem.at[slot],
            device_id=peer(me, axis, step),
            device_id_type=MESH,
        )
        copy.start()
        return copy

    sent = []

    def arrive(copies):
        for copy in copies:
            copy.wait_recv()
        sent.extend(copies)

    def fill(block, carry):
        chunk = (block % 4) * 4 + block // 4
        rows = lax.broadcasted_iota(jnp.int32, (CHUNK, LANES), 0) + chunk * CHUNK
        first = pl.multiple_of(block * CHUNK, CHUNK)
        total = jnp.zeros((CHUNK, LANES), jnp.float32)
        for group in range(GROUPS):
            signs = (2 * sign_ref[group : group + 1, :] - 1).astype(jnp.float32)
            signed = jnp.where(bucket_ref[group : group + 1, :] == rows, signs, 0.0)
            total = total + signed * res_ref[group : group + 1, :]
            hot[pl.ds(first, CHUNK), group * LANES : (group + 1) * LANES] = signed.astype(jnp.bfloat16)
        acc[pl.ds(first, CHUNK), :] = total
        return carry

    lax.fori_loop(0, SKETCH // CHUNK, fill, 0)

    def multiply(block, carry):
        first = pl.multiple_of(block * 192, 192)
        terms = jnp.dot(hot[pl.ds(first, 192), :], jac_ref[...], preferred_element_type=jnp.float32)
        for lane in range(4):
            part[lane, pl.ds(first, 192), :] = terms[:, lane * LANES : (lane + 1) * LANES]
        return carry

    lax.fori_loop(0, SKETCH // 192, multiply, 0)
    res_row = lax.dot_general(
        jnp.ones((RHS_ROWS, LANES), jnp.float32),
        acc[...],
        (((1,), (1,)), ((), ())),
        precision=HIGHEST,
        preferred_element_type=jnp.float32,
    )
    res_tile = jnp.concatenate(
        [res_row[0:1, i * LANES : (i + 1) * LANES] for i in range(BLOCKS)]
        + [jnp.zeros((RHS_ROWS - BLOCKS, LANES), jnp.float32)],
        axis=0,
    )
    for lane in range(4):
        part[lane, SKETCH:, :] = res_tile

    pl.semaphore_wait(barrier, len(links))

    x = me["x"]
    copies = [push(part.at[(x + s) % 4], x_in.at[x], "x", s) for s in (1, 2, 3)]
    x_in[x] = part[x]
    arrive(copies)
    summed = x_in[0] + x_in[1] + x_in[2] + x_in[3]
    x_sum = part.at[x]
    x_sum[...] = summed

    near = me["near"]
    copies = []
    for s in (1, 2, 3):
        rows = pl.multiple_of((near + s) % 4 * 192, 192)
        copies.append(push(x_sum.at[pl.ds(rows, 192), :], near_in.at[near, 0:192, :], "near", s))
        copies.append(push(x_sum.at[SKETCH:, :], near_in.at[near, 192:, :], "near", s))
    near_in[near, 0:192, :] = part[x, pl.ds(pl.multiple_of(near * 192, 192), 192), :]
    near_in[near, 192:, :] = part[x, SKETCH:, :]
    arrive(copies)
    near_sum = near_in.at[near]
    near_sum[...] = near_in[0] + near_in[1] + near_in[2] + near_in[3]

    far = me["far"]
    copies = []
    for s in (1, 2, 3):
        rows = pl.multiple_of((far + s) % 4 * CHUNK, CHUNK)
        copies.append(push(near_sum.at[pl.ds(rows, CHUNK), :], far_in.at[far, 0:CHUNK, :], "far", s))
        copies.append(push(near_sum.at[192:, :], far_in.at[far, CHUNK:, :], "far", s))
    far_in[far, 0:CHUNK, :] = near_in[near, pl.ds(pl.multiple_of(far * CHUNK, CHUNK), CHUNK), :]
    far_in[far, CHUNK:, :] = near_in[near, 192:, :]
    arrive(copies)
    total = (far_in[0] + far_in[1] + far_in[2] + far_in[3]) * scaling
    rhs_ref[...] = total[CHUNK:, :]
    mine = pl.multiple_of(near * 192 + far * CHUNK, CHUNK)
    cols_ref[pl.ds(mine, CHUNK), :] = total[0:CHUNK, :]
    owned_ref[x] = total[0:CHUNK, :]

    own = cols_ref.at[pl.ds(mine, CHUNK), :]
    copies = [push(own, own, "far", s) for s in (1, 2, 3)]
    owned_copies = [push(owned_ref.at[x], owned_ref.at[x], "x", s) for s in (1, 2, 3)]
    arrive(copies)
    quarter = cols_ref.at[pl.ds(pl.multiple_of(near * 192, 192), 192), :]
    copies = [push(quarter, quarter, "near", s) for s in (1, 2, 3)]
    arrive(copies)

    values = cols_ref[...]
    high = values.astype(jnp.bfloat16)
    low = (values - high.astype(jnp.float32)).astype(jnp.bfloat16)
    lhs[:, 0:LANES] = high
    lhs[:, LANES : 2 * LANES] = high
    lhs[:, 2 * LANES :] = low
    rhs_t[:, 0:LANES] = high
    rhs_t[:, LANES : 2 * LANES] = low
    rhs_t[:, 2 * LANES :] = high
    base = 0
    for i in range(BLOCKS):
        width = (i + 1) * LANES
        product = lax.dot_general(
            lhs[i * LANES : width, :],
            rhs_t[0:width, :],
            (((1,), (1,)), ((), ())),
            preferred_element_type=jnp.float32,
        )
        for j in range(i + 1):
            tri[base : base + LANES, :] = product[:, j * LANES : (j + 1) * LANES]
            base += LANES
    tri[base:, :] = jnp.zeros((TRI_ROWS - base, LANES), jnp.float32)

    core = me["core"]
    half = pl.multiple_of(core * HALF, HALF)
    other = pl.multiple_of((1 - core) * HALF, HALF)
    arrive([push(tri.at[pl.ds(other, HALF), :], core_in, "core", 1)])
    kx_out[...] = tri[pl.ds(half, HALF), :] + core_in[...]
    copies = []
    for s in (1, 2, 3):
        rows = pl.multiple_of((x + s) % 4 * X_STRIP, X_STRIP)
        copies.append(push(kx_out.at[pl.ds(rows, X_STRIP), :], kx_in.at[x], "x", s))
    kx_in[x] = kx_out[pl.ds(pl.multiple_of(x * X_STRIP, X_STRIP), X_STRIP), :]
    arrive(copies)
    ky_out[...] = kx_in[0] + kx_in[1] + kx_in[2] + kx_in[3]
    y = me["y"]
    copies = []
    for s in (1, 2, 3):
        rows = pl.multiple_of((y + s) % 4 * Y_STRIP, Y_STRIP)
        copies.append(push(ky_out.at[pl.ds(rows, Y_STRIP), :], ky_in.at[y], "y", s))
    ky_in[y] = ky_out[pl.ds(pl.multiple_of(y * Y_STRIP, Y_STRIP), Y_STRIP), :]
    arrive(copies)
    strip = pl.multiple_of(core * HALF + x * X_STRIP + y * Y_STRIP, Y_STRIP)
    tri_ref[pl.ds(strip, Y_STRIP), :] = ky_in[0] + ky_in[1] + ky_in[2] + ky_in[3]

    piece = tri_ref.at[pl.ds(strip, Y_STRIP), :]
    arrive([push(piece, piece, "y", s) for s in (1, 2, 3)])
    piece = tri_ref.at[pl.ds(pl.multiple_of(core * HALF + x * X_STRIP, X_STRIP), X_STRIP), :]
    arrive([push(piece, piece, "x", s) for s in (1, 2, 3)])
    piece = tri_ref.at[pl.ds(half, HALF), :]
    arrive([push(piece, piece, "core", 1)])
    arrive(owned_copies)
    for copy in sent:
        copy.wait_send()


COPIES = 3 + 6 + 6 + 3 + 3 + 3 + 1 + 3 + 3 + 3 + 3 + 1


def gather(jacobian, residual, bucket, sign_bit, scaling):
    f32 = jnp.float32
    return pl.pallas_call(
        functools.partial(gather_kernel, scaling),
        out_shape=(
            jax.ShapeDtypeStruct((TRI_ROWS, LANES), f32),
            jax.ShapeDtypeStruct((RHS_ROWS, LANES), f32),
            jax.ShapeDtypeStruct((SKETCH, LANES), f32),
            jax.ShapeDtypeStruct((4, CHUNK, LANES), f32),
        ),
        in_specs=[pl.BlockSpec(memory_space=pltpu.VMEM)] * 4,
        out_specs=[pl.BlockSpec(memory_space=pltpu.VMEM)] * 4,
        scratch_shapes=[
            pltpu.VMEM((SKETCH, DEV_ROWS), jnp.bfloat16),
            pltpu.VMEM((SKETCH, LANES), f32),
            pltpu.VMEM((4, SKETCH + RHS_ROWS, LANES), f32),
            pltpu.VMEM((4, SKETCH + RHS_ROWS, LANES), f32),
            pltpu.VMEM((4, 192 + RHS_ROWS, LANES), f32),
            pltpu.VMEM((4, CHUNK + RHS_ROWS, LANES), f32),
            pltpu.VMEM((SKETCH, 3 * LANES), jnp.bfloat16),
            pltpu.VMEM((SKETCH, 3 * LANES), jnp.bfloat16),
            pltpu.VMEM((TRI_ROWS, LANES), f32),
            pltpu.VMEM((HALF, LANES), f32),
            pltpu.VMEM((HALF, LANES), f32),
            pltpu.VMEM((4, X_STRIP, LANES), f32),
            pltpu.VMEM((X_STRIP, LANES), f32),
            pltpu.VMEM((4, Y_STRIP, LANES), f32),
            pltpu.SemaphoreType.DMA((COPIES,)),
            pltpu.SemaphoreType.DMA((COPIES,)),
        ],
        compiler_params=pltpu.CompilerParams(
            collective_id=0, has_side_effects=True, vmem_limit_bytes=48 * 1024 * 1024
        ),
        name="sketch_and_kernel",
    )(jacobian, residual, bucket, sign_bit)


def total_of(row):
    return jnp.sum(row, axis=(0, 1), keepdims=True)


def solve_kernel(tri_ref, rhs_ref, cols_ref, out_ref, mat, column, answer):
    base = 0
    eye = (
        lax.broadcasted_iota(jnp.int32, (LANES, LANES), 0) == lax.broadcasted_iota(jnp.int32, (LANES, LANES), 1)
    ).astype(jnp.float32) * 0.5
    for i in range(BLOCKS):
        for j in range(i + 1):
            block = tri_ref[base : base + LANES, :] * (1.0 / PARAMS)
            base += LANES
            if i == j:
                block = block + eye
            mat[i * LANES : (i + 1) * LANES, j * LANES : (j + 1) * LANES] = block
            if i != j:
                mat[j * LANES : (j + 1) * LANES, i * LANES : (i + 1) * LANES] = block.T

    raw = jnp.concatenate([rhs_ref[i : i + 1, :] for i in range(BLOCKS)], axis=1)
    largest = jnp.max(jnp.abs(raw), axis=(0, 1), keepdims=True)
    unit = jnp.where(largest > 0, largest, 1.0)
    rhs = raw / unit

    def to_column(row):
        for i in range(BLOCKS):
            piece = jnp.broadcast_to(row[:, i * LANES : (i + 1) * LANES], (LANES, LANES))
            column[i * LANES : (i + 1) * LANES, :] = piece.T

    def product(row):
        to_column(row)
        sums = [jnp.zeros((8, LANES), jnp.float32) for _ in range(BLOCKS)]
        for group in range(SKETCH // 8):
            rows = slice(group * 8, group * 8 + 8)
            weight = column[rows, :]
            for i in range(BLOCKS):
                sums[i] = sums[i] + weight * mat[rows, i * LANES : (i + 1) * LANES]
        return jnp.concatenate([jnp.sum(s, axis=0, keepdims=True) for s in sums], axis=1)

    def met(sol, res, tol):
        scale = total_of(sol * (rhs - res)) - 0.5 * total_of(sol * sol)
        return (tol * tol * scale - 2.0 * total_of(res * res))[0, 0] >= 0.0

    def step(_, carry):
        sol, res, way, size = carry
        image = product(way)
        curve = total_of(way * image)
        alpha = jnp.where(curve > 0, size / curve, 0.0)
        sol = sol + alpha * way
        res = res - alpha * image
        new_size = total_of(res * res)
        beta = jnp.where(size > 0, new_size / size, 0.0)
        return (sol, res, res + beta * way, new_size)

    def round_of(carry):
        count, _, state = carry
        state = lax.fori_loop(0, ROUND_STEPS, step, state)
        return (count + 1, met(state[0], state[1], STOP_TOL), state)

    def go_on(carry):
        count, done, _ = carry
        return jnp.logical_and(count < MAX_ROUNDS, jnp.logical_not(done))

    start = (jnp.zeros_like(rhs), rhs, rhs, total_of(rhs * rhs))
    first_done = largest[0, 0] <= 0.0
    _, _, (sol, _, _, _) = lax.while_loop(go_on, round_of, (0, first_done, start))
    true_res = rhs - product(sol)
    good = met(sol, true_res, ACCEPT_TOL)
    to_column(sol)
    answer[...] = column[...]

    @pl.when(jnp.logical_not(good))
    def _():
        to_column(rhs)
        answer[...] = column[...]
        lanes = lax.broadcasted_iota(jnp.int32, (8, SKETCH), 1)
        below = lax.broadcasted_iota(jnp.int32, (8, LANES), 0)

        def pivot(k, carry):
            pivot_row = mat[pl.ds(k, 1), :]
            pivot_rhs = answer[pl.ds(k, 1), :]
            inverse = 1.0 / jnp.sum(jnp.where(lanes[0:1] == k, pivot_row, 0.0), axis=1, keepdims=True)

            def rows_of(group, inner):
                first = pl.multiple_of(group * 8, 8)
                here = mat[pl.ds(first, 8), :]
                factor = jnp.sum(jnp.where(lanes == k, here, 0.0), axis=1, keepdims=True) * inverse
                factor = jnp.where(below[:, 0:1] + first == k, 0.0, factor)
                mat[pl.ds(first, 8), :] = here - factor * pivot_row
                answer[pl.ds(first, 8), :] = answer[pl.ds(first, 8), :] - factor * pivot_rhs
                return inner

            return lax.fori_loop(0, SKETCH // 8, rows_of, carry)

        lax.fori_loop(0, SKETCH, pivot, 0)

        def divide(group, carry):
            first = pl.multiple_of(group * 8, 8)
            here = mat[pl.ds(first, 8), :]
            row = lax.broadcasted_iota(jnp.int32, (8, SKETCH), 0) + first
            diagonal = jnp.sum(jnp.where(lanes == row, here, 0.0), axis=1, keepdims=True)
            answer[pl.ds(first, 8), :] = answer[pl.ds(first, 8), :] / diagonal
            return carry

        lax.fori_loop(0, SKETCH // 8, divide, 0)

    values = jnp.sum(answer[...] * cols_ref[...], axis=0, keepdims=True)
    out_ref[...] = jnp.broadcast_to(values * (unit * (1.0 / math.sqrt(PARAMS))), (8, LANES))


def solve(tri, rhs, cols):
    return pl.pallas_call(
        solve_kernel,
        out_shape=jax.ShapeDtypeStruct((8, LANES), jnp.float32),
        in_specs=[pl.BlockSpec(memory_space=pltpu.VMEM)] * 3,
        out_specs=pl.BlockSpec(memory_space=pltpu.VMEM),
        scratch_shapes=[
            pltpu.VMEM((SKETCH, SKETCH), jnp.float32),
            pltpu.VMEM((SKETCH, LANES), jnp.float32),
            pltpu.VMEM((SKETCH, LANES), jnp.float32),
        ],
        compiler_params=pltpu.CompilerParams(vmem_limit_bytes=48 * 1024 * 1024),
        name="solve",
    )(tri, rhs, cols)


def join_kernel(part_ref, out_ref, send_sem, recv_sem):
    me = place()
    barrier = pltpu.get_barrier_semaphore()
    for step in (1, 2, 3):
        pl.semaphore_signal(barrier, inc=1, device_id=peer(me, "x", step), device_id_type=MESH)
    x = me["x"]
    out_ref[x] = part_ref[...]
    pl.semaphore_wait(barrier, 3)
    copies = []
    for step in (1, 2, 3):
        copy = pltpu.make_async_remote_copy(
            src_ref=part_ref,
            dst_ref=out_ref.at[x],
            send_sem=send_sem.at[step - 1],
            recv_sem=recv_sem.at[step - 1],
            device_id=peer(me, "x", step),
            device_id_type=MESH,
        )
        copy.start()
        copies.append(copy)
    for copy in copies:
        copy.wait()


def join(part):
    return pl.pallas_call(
        join_kernel,
        out_shape=jax.ShapeDtypeStruct((4, 8, LANES), jnp.float32),
        in_specs=[pl.BlockSpec(memory_space=pltpu.VMEM)],
        out_specs=pl.BlockSpec(memory_space=pltpu.VMEM),
        scratch_shapes=[pltpu.SemaphoreType.DMA((3,)), pltpu.SemaphoreType.DMA((3,))],
        compiler_params=pltpu.CompilerParams(collective_id=1, has_side_effects=True),
        name="join_update",
    )(part)


def on_device(jacobian, residual, bucket, sign_bit):
    scaling = math.sqrt(SKETCH / (DEV_ROWS * 64))
    tile = (GROUPS, LANES)
    tri, rhs, cols, owned = gather(
        jacobian, residual.reshape(tile), bucket.reshape(tile), sign_bit.reshape(tile), scaling
    )
    update = join(solve(tri, rhs, cols))[:, 0, :].reshape(DEV_COLS)
    chunk = owned.transpose(1, 0, 2).reshape(CHUNK, DEV_COLS)
    rows = lax.dynamic_slice_in_dim(chunk, lax.axis_index("dp") % 4 * 12, 12, 0)
    return (update, rows)


def solution(mesh):
    return jax.shard_map(
        on_device,
        mesh=mesh,
        in_specs=(P("dp", "col"), P("dp"), P("dp"), P("dp")),
        out_specs=(P("col"), P("dp", "col")),
        check_vma=False,
    )
```

time: 731 us -> 125 us (0.17); the launches traced: 717 us -> 124 us
  waiting for transfers between devices: 291 us -> 0 us
  other arithmetic: 195 us -> 0 us
  blocking collectives: 144 us -> 0 us
  Pallas kernels: 0 us -> 117 us
  matrix products: 36.3 us -> 0 us
  local copies, waits for them, and re-layouts: 31.9 us -> 6.19 us
  between operations: 18.3 us -> 0.68 us
    psum x1 -> x0, waiting for transfers between devices: 273 us -> none  [on_device(): whole_jac, whole_res = lax.psum((partial_jac, partial_res), 'dp')]
    another operation x25 -> x0, other arithmetic: 184 us -> none  [the longest x22 124 us: on_device(): factor = jnp.linalg.cholesky(kernel)]
    psum x2 -> x0, blocking collectives: 144 us -> none  [the longest x1 113 us: on_device(): whole_jac, whole_res = lax.psum((partial_jac, partial_res), 'dp')]
    pallas_call x0 -> x3, Pallas kernels: none -> 117 us  [the longest x1 102 us: gather(): pl.pallas_call(functools.partial(gather_kernel, scaling), out_shape=(jax....]
    another operation x32 -> x0, matrix products: 24 us -> none  [the longest x10 9.81 us: on_device(): factor = jnp.linalg.cholesky(kernel)]
    all_gather x1 -> x0, waiting for transfers between devices: 18 us -> none  [on_device(): kernel = lax.all_gather(summed_rows, 'dp', axis=0, tiled=True) / PARAMS]
    another operation x27 -> x0, local copies, waits for them, and re-layouts: 16.8 us -> none
    dot_general x10 -> x0, matrix products: 12.3 us -> none  [the longest x4 7.1 us: add_block(): jnp.dot(onehot, jac_piece, preferred_element_type=jnp.float32)]
  transfers between devices with their start and end apart: 2 -> 0, of which waited for: 2 -> 0; matrix products, arithmetic and copies ran while one was open for 0% -> 0% of each run, Pallas kernels for 0% -> 0%
where the time goes in v1:
time: 125 us; the launch traced here: 124 us
  Pallas kernels  117 us (94%)
  local copies, waits for them, and re-layouts  6.19 us (5%)
    pallas_call x1, Pallas kernels, gather(): pl.pallas_call(functools.partial(gather_kernel, scaling), out_shape=(jax....  102 us
    pallas_call x1, Pallas kernels, solve(): pl.pallas_call(solve_kernel, out_shape=jax.ShapeDtypeStruct((8, LANES), j...  9.48 us
    pallas_call x1, Pallas kernels, join(): pl.pallas_call(join_kernel, out_shape=jax.ShapeDtypeStruct((4, 8, LANES),...  6.05 us
    unnamed x10, local copies, waits for them, and re-layouts  4.26 us

profile of v1, /device:TPU:1, one launch (start us, length us, event | category | flops | bytes accessed | tf_op | source)
XLA Modules:
  0.0 124.2 jit_solution(17783246518996436962)
XLA Ops:
  0.6 0.0 copy-start
  0.6 1.6 %copy-done = bf16[2048,512]{1,0:T(8,128)(2,1)S(1)} copy-done((bf16[2048,512]{1,0:T(8,128)(2,1)S(1)}, bf16[2048,512]{1,0:T(8,128)(2,1)}, u32[]{:S(2)}) %copy-start) | copy-done | bytes 2097176
  2.2 0.0 copy-start.2
  2.2 0.7 copy-done.2
  2.9 0.0 copy-start.3
  2.9 0.7 copy-done.3
  3.6 0.0 copy-start.4
  3.6 0.7 copy-done.4
  4.3 101.7 %sketch_and_kernel.1 = (f32[2816,128]{1,0:T(8,128)S(1)}, f32[8,128]{1,0:T(8,128)S(1)}, f32[768,128]{1,0:T(8,128)S(1)}, f32[4,48,128]{2,1,0:T(8,128)S(1)}) custom-call(bf16[2048,512]{1,0:T(8,128)(2,1)S(1)} %copy-done, f32[16,128]{1,0:T(8,128)S(1)} %bitcast.10, s32[16,128]{1,0:T(8,128)S(1)} %bitcast.11, s32[16,128]{1,0:T(8,128)S(1)} %bitcast.12), custom_call_target="tpu_custom_call" | custom-call | tf_op jit(solution)/shard_map/sketch_and_kernel/pallas_call | solution.py:244
  106.1 9.5 %solve.1.part_ref = f32[8,128]{1,0:T(8,128)S(1)} custom-call(f32[2816,128]{1,0:T(8,128)S(1)} %get-tuple-element.6.tri_ref, f32[8,128]{1,0:T(8,128)S(1)} %get-tuple-element.7.rhs_ref, f32[768,128]{1,0:T(8,128)S(1)} %get-tuple-element.8.cols_ref), custom_call_target="tpu_custom_call" | custom-call | tf_op jit(solution)/shard_map/solve/pallas_call | solution.py:390
  115.6 0.0 copy-start.1
  115.6 0.6 copy-done.1
  116.1 6.0 %join_update.1 = f32[4,8,128]{2,1,0:T(8,128)} custom-call(f32[8,128]{1,0:T(8,128)} %copy-done.1), custom_call_target="tpu_custom_call" | custom-call | tf_op jit(solution)/shard_map/join_update/pallas_call | solution.py:430
  122.2 1.3 %slice.3 = f32[4,1,128]{2,1,0:T(1,128)} slice(f32[4,8,128]{2,1,0:T(8,128)} %join_update.1), slice={[0:4], [0:1], [0:128]} | slice | bytes 4096 | tf_op jit(solution)/shard_map/slice | solution.py:447
  123.5 0.6 constant_dynamic-slice_fusion
  (1 shorter events, 0.0 us)
Async XLA Ops:
  0.6 1.6 %copy-start = (bf16[2048,512]{1,0:T(8,128)(2,1)S(1)}, bf16[2048,512]{1,0:T(8,128)(2,1)}, u32[]{:S(2)}) copy-start(bf16[2048,512]{1,0:T(8,128)(2,1)} %jac_ref.1) | copy-start | bytes 6291460
  2.2 0.7 copy-start.2
  2.9 0.7 copy-start.3
  3.6 0.7 copy-start.4
  115.6 0.6 copy-start.1

commit v2 on v1

v2 whole, which is shorter than its diff:
```python
import functools
import math

import jax
import jax.numpy as jnp
from jax import lax
from jax.experimental import pallas as pl
from jax.experimental.pallas import tpu as pltpu
from jax.sharding import PartitionSpec as P

PARAMS = 4096
SKETCH = 768
DEV_ROWS = 2048
DEV_COLS = 512
OWN_ROWS = 12
LANES = 128
CHUNK = 48
BLOCK = 4 * CHUNK
GROUPS = DEV_ROWS // LANES
BLOCKS = SKETCH // LANES
TRI_ROWS = 2816
HALF = TRI_ROWS // 2
PART_A = 640
PART_B = HALF - PART_A
RHS_ROWS = 8
MESH = pl.DeviceIdType.MESH
HIGHEST = lax.Precision.HIGHEST
STOP_TOL = 3e-6
ACCEPT_TOL = 1e-5
ROUND_STEPS = 4
MAX_ROUNDS = 16


def place():
    dp, col = lax.axis_index("dp"), lax.axis_index("col")
    return dict(x=dp % 4, near=(dp // 4) % 4, far=dp // 16, y=col // 2, core=col % 2)


def peer(me, axis, step):
    at = dict(me)
    size = 2 if axis == "core" else 4
    at[axis] = (me[axis] + step) % size
    return (at["far"] * 16 + at["near"] * 4 + at["x"], at["y"] * 2 + at["core"])


def gather_kernel(
    scaling,
    jac_hbm,
    res_hbm,
    bucket_hbm,
    sign_hbm,
    tri_ref,
    rhs_ref,
    cols_ref,
    jac_ref,
    res_ref,
    bucket_ref,
    sign_ref,
    hot,
    acc,
    part,
    x_in,
    x_sum,
    near_in,
    near_sum,
    far_in,
    res_x,
    res_near,
    res_far,
    lhs,
    rhs_t,
    tri,
    core_in,
    k_out,
    k_in_a,
    k_in_b,
    l_out_a,
    l_out_b,
    l_in_a,
    l_in_b,
    load_sem,
    send_sem,
    recv_sem,
):
    me = place()
    x, near, far, y, core = (me[name] for name in ("x", "near", "far", "y", "core"))
    barrier = pltpu.get_barrier_semaphore()
    links = [(axis, step) for axis in ("x", "near", "far", "y") for step in (1, 2, 3)] + [("core", 1)]
    for axis, step in links:
        pl.semaphore_signal(barrier, inc=1, device_id=peer(me, axis, step), device_id_type=MESH)

    loads = [
        pltpu.make_async_copy(src, dst, load_sem.at[i])
        for i, (src, dst) in enumerate(
            [(bucket_hbm, bucket_ref), (sign_hbm, sign_ref), (res_hbm, res_ref), (jac_hbm, jac_ref)]
        )
    ]
    for load in loads:
        load.start()

    used = [0]
    sent = []

    def push(src, dst, axis, step):
        slot = used[0]
        used[0] += 1
        copy = pltpu.make_async_remote_copy(
            src_ref=src,
            dst_ref=dst,
            send_sem=send_sem.at[slot],
            recv_sem=recv_sem.at[slot],
            device_id=peer(me, axis, step),
            device_id_type=MESH,
        )
        copy.start()
        sent.append(copy)
        return copy

    def arrive(copies):
        for copy in copies:
            copy.wait_recv()

    def rows_at(first, count, unit=8):
        return pl.ds(pl.multiple_of(first, unit), count)

    def block_at(index):
        return rows_at(index % 4 * BLOCK, BLOCK, BLOCK)

    for load in loads[:3]:
        load.wait()

    def fill(block, carry):
        chunk = (block % 4) * 4 + block // 4
        rows = lax.broadcasted_iota(jnp.int32, (CHUNK, LANES), 0) + chunk * CHUNK
        first = pl.multiple_of(block * CHUNK, CHUNK)
        total = jnp.zeros((CHUNK, LANES), jnp.float32)
        for group in range(GROUPS):
            signs = (2 * sign_ref[group : group + 1, :] - 1).astype(jnp.float32)
            signed = jnp.where(bucket_ref[group : group + 1, :] == rows, signs, 0.0)
            total = total + signed * res_ref[group : group + 1, :]
            hot[pl.ds(first, CHUNK), group * LANES : (group + 1) * LANES] = signed.astype(jnp.bfloat16)
        acc[pl.ds(first, CHUNK), :] = total
        return carry

    lax.fori_loop(0, SKETCH // CHUNK, fill, 0)
    loads[3].wait()

    def multiply(block, carry):
        first = pl.multiple_of(block * BLOCK, BLOCK)
        terms = jnp.dot(hot[pl.ds(first, BLOCK), :], jac_ref[...], preferred_element_type=jnp.float32)
        for lane in range(4):
            part[lane, pl.ds(first, BLOCK), :] = terms[:, lane * LANES : (lane + 1) * LANES]
        return carry

    lax.fori_loop(0, SKETCH // BLOCK, multiply, 0)
    pl.semaphore_wait(barrier, len(links))

    x_copies = []
    for q in range(4):
        rows = block_at(near + 1 + q)
        x_copies.append([push(part.at[(x + s) % 4, rows, :], x_in.at[x, rows, :], "x", s) for s in (2, 1, 3)])

    res_row = lax.dot_general(
        jnp.ones((RHS_ROWS, LANES), jnp.float32),
        acc[...],
        (((1,), (1,)), ((), ())),
        precision=HIGHEST,
        preferred_element_type=jnp.float32,
    )
    res_x[x] = jnp.concatenate(
        [res_row[0:1, i * LANES : (i + 1) * LANES] for i in range(BLOCKS)]
        + [jnp.zeros((RHS_ROWS - BLOCKS, LANES), jnp.float32)],
        axis=0,
    )
    res_copies = [push(res_x.at[x], res_x.at[x], "x", s) for s in (1, 2, 3)]

    near_copies = []
    for q in range(4):
        rows = block_at(near + 1 + q)
        arrive(x_copies[q])
        summed = part[x, rows, :]
        for s in (1, 2, 3):
            summed = summed + x_in[(x + s) % 4, rows, :]
        if q < 3:
            x_sum[rows, :] = summed
            near_copies.append(push(x_sum.at[rows, :], near_in.at[near], "near", q + 1))
        else:
            near_in[near] = summed
        if q == 1:
            arrive(res_copies)
            res_near[near] = res_x[0] + res_x[1] + res_x[2] + res_x[3]
            res_copies = [push(res_near.at[near], res_near.at[near], "near", s) for s in (1, 2, 3)]
    arrive(near_copies)
    near_sum[...] = near_in[0] + near_in[1] + near_in[2] + near_in[3]

    far_copies = []
    for s in (2, 1, 3):
        rows = rows_at((far + s) % 4 * CHUNK, CHUNK, CHUNK)
        far_copies.append(push(near_sum.at[rows, :], far_in.at[far], "far", s))
    far_in[far] = near_sum[rows_at(far * CHUNK, CHUNK, CHUNK), :]
    arrive(res_copies)
    res_far[far] = res_near[0] + res_near[1] + res_near[2] + res_near[3]
    res_copies = [push(res_far.at[far], res_far.at[far], "far", s) for s in (1, 2, 3)]
    arrive(far_copies)

    def chunk_of(at_near, at_far):
        rows = rows_at(at_near % 4 * BLOCK + at_far % 4 * CHUNK, CHUNK, CHUNK)
        return cols_ref.at[x, rows, :]

    own = chunk_of(near, far)
    own[...] = (far_in[0] + far_in[1] + far_in[2] + far_in[3]) * scaling

    far_copies = {s: push(own, own, "far", s) for s in (2, 1, 3)}
    near_copies = [push(own, own, "near", s) for s in (2, 1, 3)]
    cols_copies = [push(own, own, "x", s) for s in (2, 1, 3)]
    arrive(res_copies)
    rhs_ref[...] = (res_far[0] + res_far[1] + res_far[2] + res_far[3]) * scaling
    for s in (1, 3, 2):
        arrive([far_copies[s]])
        chunk = chunk_of(near, far - s + 4)
        near_copies += [push(chunk, chunk, "near", t) for t in (2, 1, 3)]
        cols_copies += [push(chunk, chunk, "x", t) for t in (2, 1, 3)]
    arrive(near_copies)

    def share(step):
        block = cols_ref.at[x, block_at(near + step), :]
        cols_copies.extend([push(block, block, "x", t) for t in (2, 1, 3)])

    share(1)

    values = cols_ref[x]
    high = values.astype(jnp.bfloat16)
    low = (values - high.astype(jnp.float32)).astype(jnp.bfloat16)
    lhs[:, 0:LANES] = high
    lhs[:, LANES : 2 * LANES] = high
    lhs[:, 2 * LANES :] = low
    rhs_t[:, 0:LANES] = high
    rhs_t[:, LANES : 2 * LANES] = low
    rhs_t[:, 2 * LANES :] = high
    base = 0
    for i in range(BLOCKS):
        width = (i + 1) * LANES
        product = lax.dot_general(
            lhs[i * LANES : width, :],
            rhs_t[0:width, :],
            (((1,), (1,)), ((), ())),
            preferred_element_type=jnp.float32,
        )
        for j in range(i + 1):
            tri[base : base + LANES, :] = product[:, j * LANES : (j + 1) * LANES]
            base += LANES
    tri[base:, :] = jnp.zeros((TRI_ROWS - base, LANES), jnp.float32)

    half = core * HALF
    other = (1 - core) * HALF
    spans = ((0, PART_A), (PART_A, PART_B))
    core_copies = [
        push(tri.at[rows_at(other + first, count), :], core_in.at[first : first + count, :], "core", 1)
        for first, count in spans
    ]
    orders = (("x", "y", x, y, k_in_a, l_out_a, l_in_a), ("y", "x", y, x, k_in_b, l_out_b, l_in_b))

    first_copies = []
    for (first, count), copy, (axis, _, index, _, k_in, _, _) in zip(spans, core_copies, orders):
        arrive([copy])
        k_out[first : first + count, :] = tri[rows_at(half + first, count), :] + core_in[first : first + count, :]
        strip = count // 4
        first_copies.append(
            [
                push(k_out.at[rows_at(first + (index + s) % 4 * strip, strip), :], k_in.at[index], axis, s)
                for s in (2, 1, 3)
            ]
        )
        k_in[index] = k_out[rows_at(first + index * strip, strip), :]
    second_copies = []
    for (first, count), copies, (_, axis, _, index, k_in, l_out, l_in) in zip(spans, first_copies, orders):
        strip = count // 16
        arrive(copies)
        l_out[...] = k_in[0] + k_in[1] + k_in[2] + k_in[3]
        second_copies.append(
            [push(l_out.at[rows_at((index + s) % 4 * strip, strip), :], l_in.at[index], axis, s) for s in (2, 1, 3)]
        )
        l_in[index] = l_out[rows_at(index * strip, strip), :]
    share(2)
    second_back = []
    for (first, count), copies, (_, axis, outer, inner, _, _, l_in) in zip(spans, second_copies, orders):
        strip = count // 16
        arrive(copies)
        piece = tri_ref.at[rows_at(half + first + outer * (count // 4) + inner * strip, strip), :]
        piece[...] = l_in[0] + l_in[1] + l_in[2] + l_in[3]
        second_back.append([push(piece, piece, axis, s) for s in (2, 1, 3)])
    share(3)

    def quarter(first, count, index):
        return tri_ref.at[rows_at(half + first + index % 4 * (count // 4), count // 4), :]

    first_back = []
    last_copies = []
    for (first, count), copies, (axis, _, outer, _, _, _, _) in zip(spans, second_back, orders):
        arrive(copies)
        piece = quarter(first, count, outer)
        first_back.append([push(piece, piece, axis, s) for s in (2, 1, 3)])
        last_copies.append(push(piece, piece, "core", 1))
    for (first, count), copies, (_, _, outer, _, _, _, _) in zip(spans, first_back, orders):
        for s, copy in zip((2, 1, 3), copies):
            arrive([copy])
            piece = quarter(first, count, outer - s + 4)
            last_copies.append(push(piece, piece, "core", 1))
    assert used[0] == COPIES
    arrive(last_copies)
    arrive(cols_copies)
    for copy in sent:
        copy.wait_send()


COPIES = 97


def gather(jacobian, residual, bucket, sign_bit, scaling):
    f32 = jnp.float32
    shapes = [
        ((DEV_ROWS, DEV_COLS), jnp.bfloat16),
        ((GROUPS, LANES), f32),
        ((GROUPS, LANES), jnp.int32),
        ((GROUPS, LANES), jnp.int32),
        ((SKETCH, DEV_ROWS), jnp.bfloat16),
        ((SKETCH, LANES), f32),
        ((4, SKETCH, LANES), f32),
        ((4, SKETCH, LANES), f32),
        ((SKETCH, LANES), f32),
        ((4, BLOCK, LANES), f32),
        ((BLOCK, LANES), f32),
        ((4, CHUNK, LANES), f32),
        ((4, RHS_ROWS, LANES), f32),
        ((4, RHS_ROWS, LANES), f32),
        ((4, RHS_ROWS, LANES), f32),
        ((SKETCH, 3 * LANES), jnp.bfloat16),
        ((SKETCH, 3 * LANES), jnp.bfloat16),
        ((TRI_ROWS, LANES), f32),
        ((HALF, LANES), f32),
        ((HALF, LANES), f32),
        ((4, PART_A // 4, LANES), f32),
        ((4, PART_B // 4, LANES), f32),
        ((PART_A // 4, LANES), f32),
        ((PART_B // 4, LANES), f32),
        ((4, PART_A // 16, LANES), f32),
        ((4, PART_B // 16, LANES), f32),
    ]
    return pl.pallas_call(
        functools.partial(gather_kernel, scaling),
        out_shape=(
            jax.ShapeDtypeStruct((TRI_ROWS, LANES), f32),
            jax.ShapeDtypeStruct((RHS_ROWS, LANES), f32),
            jax.ShapeDtypeStruct((4, SKETCH, LANES), f32),
        ),
        in_specs=[pl.BlockSpec(memory_space=pl.ANY)] * 4,
        out_specs=[pl.BlockSpec(memory_space=pltpu.VMEM)] * 3,
        scratch_shapes=[pltpu.VMEM(shape, kind) for shape, kind in shapes]
        + [
            pltpu.SemaphoreType.DMA((4,)),
            pltpu.SemaphoreType.DMA((COPIES,)),
            pltpu.SemaphoreType.DMA((COPIES,)),
        ],
        compiler_params=pltpu.CompilerParams(
            collective_id=0, has_side_effects=True, vmem_limit_bytes=56 * 1024 * 1024
        ),
        name="sketch_and_kernel",
    )(jacobian, residual, bucket, sign_bit)


def total_of(row):
    return jnp.sum(row, axis=(0, 1), keepdims=True)


def solve_kernel(tri_ref, rhs_ref, cols_ref, out_ref, mat, column, answer):
    base = 0
    eye = (
        lax.broadcasted_iota(jnp.int32, (LANES, LANES), 0) == lax.broadcasted_iota(jnp.int32, (LANES, LANES), 1)
    ).astype(jnp.float32) * 0.5
    for i in range(BLOCKS):
        for j in range(i + 1):
            block = tri_ref[base : base + LANES, :] * (1.0 / PARAMS)
            base += LANES
            if i == j:
                block = block + eye
            mat[i * LANES : (i + 1) * LANES, j * LANES : (j + 1) * LANES] = block
            if i != j:
                mat[j * LANES : (j + 1) * LANES, i * LANES : (i + 1) * LANES] = block.T

    raw = jnp.concatenate([rhs_ref[i : i + 1, :] for i in range(BLOCKS)], axis=1)
    largest = jnp.max(jnp.abs(raw), axis=(0, 1), keepdims=True)
    unit = jnp.where(largest > 0, largest, 1.0)
    rhs = raw / unit

    def to_column(row):
        for i in range(BLOCKS):
            piece = jnp.broadcast_to(row[:, i * LANES : (i + 1) * LANES], (LANES, LANES))
            column[i * LANES : (i + 1) * LANES, :] = piece.T

    def product(row):
        to_column(row)
        sums = [jnp.zeros((8, LANES), jnp.float32) for _ in range(BLOCKS)]
        for group in range(SKETCH // 8):
            rows = slice(group * 8, group * 8 + 8)
            weight = column[rows, :]
            for i in range(BLOCKS):
                sums[i] = sums[i] + weight * mat[rows, i * LANES : (i + 1) * LANES]
        return jnp.concatenate([jnp.sum(s, axis=0, keepdims=True) for s in sums], axis=1)

    def met(sol, res, tol):
        scale = total_of(sol * (rhs - res)) - 0.5 * total_of(sol * sol)
        return (tol * tol * scale - 2.0 * total_of(res * res))[0, 0] >= 0.0

    def step(_, carry):
        sol, res, way, size = carry
        image = product(way)
        curve = total_of(way * image)
        alpha = jnp.where(curve > 0, size / curve, 0.0)
        sol = sol + alpha * way
        res = res - alpha * image
        new_size = total_of(res * res)
        beta = jnp.where(size > 0, new_size / size, 0.0)
        return (sol, res, res + beta * way, new_size)

    def round_of(carry):
        count, _, state = carry
        state = lax.fori_loop(0, ROUND_STEPS, step, state)
        return (count + 1, met(state[0], state[1], STOP_TOL), state)

    def go_on(carry):
        count, done, _ = carry
        return jnp.logical_and(count < MAX_ROUNDS, jnp.logical_not(done))

    start = (jnp.zeros_like(rhs), rhs, rhs, total_of(rhs * rhs))
    first_done = largest[0, 0] <= 0.0
    _, _, (sol, _, _, _) = lax.while_loop(go_on, round_of, (0, first_done, start))
    true_res = rhs - product(sol)
    good = met(sol, true_res, ACCEPT_TOL)
    to_column(sol)
    answer[...] = column[...]

    @pl.when(jnp.logical_not(good))
    def _():
        to_column(rhs)
        answer[...] = column[...]
        lanes = lax.broadcasted_iota(jnp.int32, (8, SKETCH), 1)
        below = lax.broadcasted_iota(jnp.int32, (8, LANES), 0)

        def pivot(k, carry):
            pivot_row = mat[pl.ds(k, 1), :]
            pivot_rhs = answer[pl.ds(k, 1), :]
            inverse = 1.0 / jnp.sum(jnp.where(lanes[0:1] == k, pivot_row, 0.0), axis=1, keepdims=True)

            def rows_of(group, inner):
                first = pl.multiple_of(group * 8, 8)
                here = mat[pl.ds(first, 8), :]
                factor = jnp.sum(jnp.where(lanes == k, here, 0.0), axis=1, keepdims=True) * inverse
                factor = jnp.where(below[:, 0:1] + first == k, 0.0, factor)
                mat[pl.ds(first, 8), :] = here - factor * pivot_row
                answer[pl.ds(first, 8), :] = answer[pl.ds(first, 8), :] - factor * pivot_rhs
                return inner

            return lax.fori_loop(0, SKETCH // 8, rows_of, carry)

        lax.fori_loop(0, SKETCH, pivot, 0)

        def divide(group, carry):
            first = pl.multiple_of(group * 8, 8)
            here = mat[pl.ds(first, 8), :]
            row = lax.broadcasted_iota(jnp.int32, (8, SKETCH), 0) + first
            diagonal = jnp.sum(jnp.where(lanes == row, here, 0.0), axis=1, keepdims=True)
            answer[pl.ds(first, 8), :] = answer[pl.ds(first, 8), :] / diagonal
            return carry

        lax.fori_loop(0, SKETCH // 8, divide, 0)

    for lane in range(4):
        values = jnp.sum(answer[...] * cols_ref[lane], axis=0, keepdims=True)
        out_ref[:, lane * LANES : (lane + 1) * LANES] = values * (unit * (1.0 / math.sqrt(PARAMS)))


def solve(tri, rhs, cols):
    return pl.pallas_call(
        solve_kernel,
        out_shape=jax.ShapeDtypeStruct((1, DEV_COLS), jnp.float32),
        in_specs=[pl.BlockSpec(memory_space=pltpu.VMEM)] * 3,
        out_specs=pl.BlockSpec(memory_space=pltpu.VMEM),
        scratch_shapes=[
            pltpu.VMEM((SKETCH, SKETCH), jnp.float32),
            pltpu.VMEM((SKETCH, LANES), jnp.float32),
            pltpu.VMEM((SKETCH, LANES), jnp.float32),
        ],
        compiler_params=pltpu.CompilerParams(vmem_limit_bytes=48 * 1024 * 1024),
        name="solve",
    )(tri, rhs, cols)


def on_device(jacobian, residual, bucket, sign_bit):
    scaling = math.sqrt(SKETCH / (DEV_ROWS * 64))
    tile = (GROUPS, LANES)
    tri, rhs, cols = gather(
        jacobian, residual.reshape(tile), bucket.reshape(tile), sign_bit.reshape(tile), scaling
    )
    update = solve(tri, rhs, cols).reshape(DEV_COLS)
    me = place()
    first = me["near"] * BLOCK + me["far"] * CHUNK + me["x"] * OWN_ROWS
    mine = lax.dynamic_slice_in_dim(cols, first, OWN_ROWS, 1)
    rows = mine.transpose(1, 0, 2).reshape(OWN_ROWS, DEV_COLS)
    return (update, rows)


def solution(mesh):
    return jax.shard_map(
        on_device,
        mesh=mesh,
        in_specs=(P("dp", "col"), P("dp"), P("dp"), P("dp")),
        out_specs=(P("col"), P("dp", "col")),
        check_vma=False,
    )
```

time: 125 us -> 108 us (0.86)
  Pallas kernels: 117 us -> 102 us
  local copies, waits for them, and re-layouts: 6.19 us -> 4.89 us
    pallas_call x1, Pallas kernels: 102 us -> 91.9 us  [gather(): pl.pallas_call(functools.partial(gather_kernel, scaling), out_shape=(jax....]
    pallas_call x2 -> x1, Pallas kernels: 15.5 us -> 10.2 us  [solve(): pl.pallas_call(solve_kernel, out_shape=jax.ShapeDtypeStruct((1, DEV_COLS)...]
    slice x1 -> x0, local copies, waits for them, and re-layouts: 1.3 us -> none  [on_device(): update = join(solve(tri, rhs, cols))[:, 0, :].reshape(DEV_COLS)]
    unnamed x10 -> x8, local copies, waits for them, and re-layouts: 4.26 us -> 4.07 us
where the time goes in v2:
time: 108 us
  Pallas kernels  102 us (94%)
  local copies, waits for them, and re-layouts  4.89 us (5%)
    pallas_call x1, Pallas kernels, gather(): pl.pallas_call(functools.partial(gather_kernel, scaling), out_shape=(jax....  91.9 us
    pallas_call x1, Pallas kernels, solve(): pl.pallas_call(solve_kernel, out_shape=jax.ShapeDtypeStruct((1, DEV_COLS)...  10.2 us
    unnamed x8, local copies, waits for them, and re-layouts  4.07 us

profile of v2, /device:TPU:1, one launch (start us, length us, event | category | flops | bytes accessed | tf_op | source)
XLA Modules:
  0.0 107.6 jit_solution(9141027006988224363)
XLA Ops:
  0.6 91.9 %sketch_and_kernel.1 = (f32[2816,128]{1,0:T(8,128)}, f32[8,128]{1,0:T(8,128)}, f32[4,768,128]{2,1,0:T(8,128)}) custom-call(bf16[2048,512]{1,0:T(8,128)(2,1)} %jac_hbm.1, f32[16,128]{1,0:T(8,128)} %bitcast.11, s32[16,128]{1,0:T(8,128)} %bitcast.12, s32[16,128]{1,0:T(8,128)} %bitcast.13), custom_call_target="tpu_custom_call" | custom-call | tf_op jit(solution)/shard_map/sketch_and_kernel/pallas_call | solution.py:349
  92.6 0.0 copy-start
  92.6 1.4 %copy-done = f32[4,768,128]{2,1,0:T(8,128)S(1)} copy-done((f32[4,768,128]{2,1,0:T(8,128)S(1)}, f32[4,768,128]{2,1,0:T(8,128)}, u32[]{:S(2)}) %copy-start) | copy-done | bytes 1572888
  94.0 0.0 copy-start.1
  94.0 1.4 %copy-done.1 = f32[2816,128]{1,0:T(8,128)S(1)} copy-done((f32[2816,128]{1,0:T(8,128)S(1)}, f32[2816,128]{1,0:T(8,128)}, u32[]{:S(2)}) %copy-start.1) | copy-done | bytes 1441816
  95.3 0.0 copy-start.2
  95.3 0.7 copy-done.2
  96.0 10.2 %solve.1 = f32[1,512]{1,0:T(1,128)} custom-call(f32[2816,128]{1,0:T(8,128)S(1)} %copy-done.1, f32[8,128]{1,0:T(8,128)S(1)} %copy-done.2, f32[4,768,128]{2,1,0:T(8,128)S(1)} %copy-done), custom_call_target="tpu_custom_call" | custom-call | tf_op jit(solution)/shard_map/solve/pallas_call | solution.py:483
  106.2 0.8 dynamic-slice_bitcast_fusion
  107.0 0.6 copy.7
  (2 shorter events, 0.0 us)
Async XLA Ops:
  92.6 1.4 %copy-start = (f32[4,768,128]{2,1,0:T(8,128)S(1)}, f32[4,768,128]{2,1,0:T(8,128)}, u32[]{:S(2)}) copy-start(f32[4,768,128]{2,1,0:T(8,128)} %get-tuple-element.7.cols_ref) | copy-start | bytes 4718596
  94.0 1.4 %copy-start.1 = (f32[2816,128]{1,0:T(8,128)S(1)}, f32[2816,128]{1,0:T(8,128)}, u32[]{:S(2)}) copy-start(f32[2816,128]{1,0:T(8,128)} %get-tuple-element.5.tri_ref) | copy-start | bytes 4325380
  95.3 0.7 copy-start.2

commit v3 on v2

--- a/solution.py
+++ b/solution.py
@@ -46,16 +46,12 @@
 def gather_kernel(
     scaling,
     jac_hbm,
-    res_hbm,
-    bucket_hbm,
-    sign_hbm,
+    coded_ref,
+    res_ref,
     tri_ref,
     rhs_ref,
     cols_ref,
     jac_ref,
-    res_ref,
-    bucket_ref,
-    sign_ref,
     hot,
     acc,
     part,
@@ -89,14 +85,8 @@
     for axis, step in links:
         pl.semaphore_signal(barrier, inc=1, device_id=peer(me, axis, step), device_id_type=MESH)
 
-    loads = [
-        pltpu.make_async_copy(src, dst, load_sem.at[i])
-        for i, (src, dst) in enumerate(
-            [(bucket_hbm, bucket_ref), (sign_hbm, sign_ref), (res_hbm, res_ref), (jac_hbm, jac_ref)]
-        )
-    ]
-    for load in loads:
-        load.start()
+    load = pltpu.make_async_copy(jac_hbm, jac_ref, load_sem)
+    load.start()
 
     used = [0]
     sent = []
@@ -126,38 +116,31 @@
     def block_at(index):
         return rows_at(index % 4 * BLOCK, BLOCK, BLOCK)
 
-    for load in loads[:3]:
-        load.wait()
-
     def fill(block, carry):
         chunk = (block % 4) * 4 + block // 4
-        rows = lax.broadcasted_iota(jnp.int32, (CHUNK, LANES), 0) + chunk * CHUNK
+        targets = (lax.broadcasted_iota(jnp.int32, (CHUNK, LANES), 0) + chunk * CHUNK + 1).astype(jnp.float32)
         first = pl.multiple_of(block * CHUNK, CHUNK)
         total = jnp.zeros((CHUNK, LANES), jnp.float32)
         for group in range(GROUPS):
-            signs = (2 * sign_ref[group : group + 1, :] - 1).astype(jnp.float32)
-            signed = jnp.where(bucket_ref[group : group + 1, :] == rows, signs, 0.0)
-            total = total + signed * res_ref[group : group + 1, :]
+            code = coded_ref[group : group + 1, :]
+            hit = jnp.abs(code) == targets
+            total = total + jnp.where(hit, res_ref[group : group + 1, :], 0.0)
+            signed = jnp.where(hit, jnp.where(code > 0.0, 1.0, -1.0), 0.0)
             hot[pl.ds(first, CHUNK), group * LANES : (group + 1) * LANES] = signed.astype(jnp.bfloat16)
         acc[pl.ds(first, CHUNK), :] = total
         return carry
 
     lax.fori_loop(0, SKETCH // CHUNK, fill, 0)
-    loads[3].wait()
-
-    def multiply(block, carry):
-        first = pl.multiple_of(block * BLOCK, BLOCK)
-        terms = jnp.dot(hot[pl.ds(first, BLOCK), :], jac_ref[...], preferred_element_type=jnp.float32)
-        for lane in range(4):
-            part[lane, pl.ds(first, BLOCK), :] = terms[:, lane * LANES : (lane + 1) * LANES]
-        return carry
-
-    lax.fori_loop(0, SKETCH // BLOCK, multiply, 0)
-    pl.semaphore_wait(barrier, len(links))
+    load.wait()
 
     x_copies = []
     for q in range(4):
         rows = block_at(near + 1 + q)
+        terms = jnp.dot(hot[rows, :], jac_ref[...], preferred_element_type=jnp.float32)
+        for lane in range(4):
+            part[lane, rows, :] = terms[:, lane * LANES : (lane + 1) * LANES]
+        if q == 0:
+            pl.semaphore_wait(barrier, len(links))
         x_copies.append([push(part.at[(x + s) % 4, rows, :], x_in.at[x, rows, :], "x", s) for s in (2, 1, 3)])
 
     res_row = lax.dot_general(
@@ -316,13 +299,10 @@
 COPIES = 97
 
 
-def gather(jacobian, residual, bucket, sign_bit, scaling):
+def gather(jacobian, coded, residual, scaling):
     f32 = jnp.float32
     shapes = [
         ((DEV_ROWS, DEV_COLS), jnp.bfloat16),
-        ((GROUPS, LANES), f32),
-        ((GROUPS, LANES), jnp.int32),
-        ((GROUPS, LANES), jnp.int32),
         ((SKETCH, DEV_ROWS), jnp.bfloat16),
         ((SKETCH, LANES), f32),
         ((4, SKETCH, LANES), f32),
@@ -353,26 +333,35 @@
             jax.ShapeDtypeStruct((RHS_ROWS, LANES), f32),
             jax.ShapeDtypeStruct((4, SKETCH, LANES), f32),
         ),
-        in_specs=[pl.BlockSpec(memory_space=pl.ANY)] * 4,
+        in_specs=[pl.BlockSpec(memory_space=pl.ANY), pl.BlockSpec(memory_space=pltpu.VMEM), pl.BlockSpec(memory_space=pltpu.VMEM)],
         out_specs=[pl.BlockSpec(memory_space=pltpu.VMEM)] * 3,
         scratch_shapes=[pltpu.VMEM(shape, kind) for shape, kind in shapes]
         + [
-            pltpu.SemaphoreType.DMA((4,)),
+            pltpu.SemaphoreType.DMA,
             pltpu.SemaphoreType.DMA((COPIES,)),
             pltpu.SemaphoreType.DMA((COPIES,)),
         ],
         compiler_params=pltpu.CompilerParams(
-            collective_id=0, has_side_effects=True, vmem_limit_bytes=56 * 1024 * 1024
+            collective_id=0, has_side_effects=True, vmem_limit_bytes=50 * 1024 * 1024
         ),
         name="sketch_and_kernel",
-    )(jacobian, residual, bucket, sign_bit)
+    )(jacobian, coded, residual)
 
 
 def total_of(row):
     return jnp.sum(row, axis=(0, 1), keepdims=True)
 
 
-def solve_kernel(tri_ref, rhs_ref, cols_ref, out_ref, mat, column, answer):
+def solve_kernel(tri_ref, rhs_ref, cols_ref, out_ref, rows_ref, mat, column, answer):
+    me = place()
+    first = pl.multiple_of(me["near"] * BLOCK + me["far"] * CHUNK, CHUNK)
+    for lane in range(4):
+        chunk = cols_ref[lane, pl.ds(first, CHUNK), :]
+        mine = chunk[:OWN_ROWS]
+        for i in range(1, 4):
+            mine = jnp.where(me["x"] == i, chunk[i * OWN_ROWS : (i + 1) * OWN_ROWS], mine)
+        rows_ref[:, lane * LANES : (lane + 1) * LANES] = mine
+
     base = 0
     eye = (
         lax.broadcasted_iota(jnp.int32, (LANES, LANES), 0) == lax.broadcasted_iota(jnp.int32, (LANES, LANES), 1)
@@ -482,15 +471,18 @@
 def solve(tri, rhs, cols):
     return pl.pallas_call(
         solve_kernel,
-        out_shape=jax.ShapeDtypeStruct((1, DEV_COLS), jnp.float32),
+        out_shape=(
+            jax.ShapeDtypeStruct((1, DEV_COLS), jnp.float32),
+            jax.ShapeDtypeStruct((OWN_ROWS, DEV_COLS), jnp.float32),
+        ),
         in_specs=[pl.BlockSpec(memory_space=pltpu.VMEM)] * 3,
-        out_specs=pl.BlockSpec(memory_space=pltpu.VMEM),
+        out_specs=[pl.BlockSpec(memory_space=pltpu.VMEM)] * 2,
         scratch_shapes=[
             pltpu.VMEM((SKETCH, SKETCH), jnp.float32),
             pltpu.VMEM((SKETCH, LANES), jnp.float32),
             pltpu.VMEM((SKETCH, LANES), jnp.float32),
         ],
-        compiler_params=pltpu.CompilerParams(vmem_limit_bytes=48 * 1024 * 1024),
+        compiler_params=pltpu.CompilerParams(vmem_limit_bytes=16 * 1024 * 1024),
         name="solve",
     )(tri, rhs, cols)
 
@@ -498,15 +490,11 @@
 def on_device(jacobian, residual, bucket, sign_bit):
     scaling = math.sqrt(SKETCH / (DEV_ROWS * 64))
     tile = (GROUPS, LANES)
-    tri, rhs, cols = gather(
-        jacobian, residual.reshape(tile), bucket.reshape(tile), sign_bit.reshape(tile), scaling
-    )
-    update = solve(tri, rhs, cols).reshape(DEV_COLS)
-    me = place()
-    first = me["near"] * BLOCK + me["far"] * CHUNK + me["x"] * OWN_ROWS
-    mine = lax.dynamic_slice_in_dim(cols, first, OWN_ROWS, 1)
-    rows = mine.transpose(1, 0, 2).reshape(OWN_ROWS, DEV_COLS)
-    return (update, rows)
+    signs = (2 * sign_bit - 1).astype(jnp.float32)
+    coded = (bucket.astype(jnp.float32) + 1.0) * signs
+    tri, rhs, cols = gather(jacobian, coded.reshape(tile), (residual * signs).reshape(tile), scaling)
+    update, rows = solve(tri, rhs, cols)
+    return (update.reshape(DEV_COLS), rows)
 
 
 def solution(mesh):

time: 108 us -> 103 us (0.954)
  local copies, waits for them, and re-layouts: 4.89 us -> 0 us
    unnamed x8 -> x0, local copies, waits for them, and re-layouts: 4.07 us -> none
where the time goes in v3:
time: 103 us; the launch traced here: 102 us
  Pallas kernels  101 us (98%)
    pallas_call x1, Pallas kernels, gather(): pl.pallas_call(functools.partial(gather_kernel, scaling), out_shape=(jax....  90.9 us
    pallas_call x1, Pallas kernels, solve(): pl.pallas_call(solve_kernel, out_shape=(jax.ShapeDtypeStruct((1, DEV_COLS...  10.2 us

profile of v3, /device:TPU:1, one launch (start us, length us, event | category | flops | bytes accessed | tf_op | source)
XLA Modules:
  0.0 102.4 jit_solution(17625339165373488312)
XLA Ops:
  0.6 0.7 multiply_bitcast_fusion
  1.4 90.9 %sketch_and_kernel.1 = (f32[2816,128]{1,0:T(8,128)S(1)}, f32[8,128]{1,0:T(8,128)S(1)}, f32[4,768,128]{2,1,0:T(8,128)S(1)}) custom-call(bf16[2048,512]{1,0:T(8,128)(2,1)} %jac_hbm.1, f32[16,128]{1,0:T(8,128)S(1)} %get-tuple-element.13.coded_ref, f32[16,128]{1,0:T(8,128)S(1)} %get-tuple-element.12.res_ref), custom_call_target="tpu_custom_call" | custom-call | tf_op jit(solution)/shard_map/sketch_and_kernel/pallas_call | solution.py:329
  92.3 10.2 %solve.1 = (f32[1,512]{1,0:T(1,128)}, f32[12,512]{1,0:T(8,128)}) custom-call(f32[2816,128]{1,0:T(8,128)S(1)} %get-tuple-element.7.tri_ref, f32[8,128]{1,0:T(8,128)S(1)} %get-tuple-element.8.rhs_ref, f32[4,768,128]{2,1,0:T(8,128)S(1)} %get-tuple-element.9.cols_ref), custom_call_target="tpu_custom_call" | custom-call | tf_op jit(solution)/shard_map/solve/pallas_call | solution.py:472

commit v4 on v3

--- a/solution.py
+++ b/solution.py
@@ -43,6 +43,11 @@
     return (at["far"] * 16 + at["near"] * 4 + at["x"], at["y"] * 2 + at["core"])
 
 
+def along_z(me, step):
+    z = (me["far"] * 4 + me["near"] + step + 16) % 16
+    return (z * 4 + me["x"], me["y"] * 2 + me["core"])
+
+
 def gather_kernel(
     scaling,
     jac_hbm,
@@ -55,6 +60,7 @@
     hot,
     acc,
     part,
+    fold_in,
     x_in,
     x_sum,
     near_in,
@@ -74,6 +80,7 @@
     l_out_b,
     l_in_a,
     l_in_b,
+    known_sem,
     load_sem,
     send_sem,
     recv_sem,
@@ -81,9 +88,14 @@
     me = place()
     x, near, far, y, core = (me[name] for name in ("x", "near", "far", "y", "core"))
     barrier = pltpu.get_barrier_semaphore()
-    links = [(axis, step) for axis in ("x", "near", "far", "y") for step in (1, 2, 3)] + [("core", 1)]
-    for axis, step in links:
-        pl.semaphore_signal(barrier, inc=1, device_id=peer(me, axis, step), device_id_type=MESH)
+    beside = [peer(me, axis, step) for axis, step in (("x", 1), ("x", 3), ("y", 1), ("y", 3), ("core", 1))]
+    beside += [along_z(me, 1), along_z(me, -1)]
+    for device in beside:
+        pl.semaphore_signal(barrier, inc=1, device_id=device, device_id_type=MESH)
+
+    def vouch(level, devices):
+        for device in devices:
+            pl.semaphore_signal(known_sem.at[level], inc=1, device_id=device, device_id_type=MESH)
 
     load = pltpu.make_async_copy(jac_hbm, jac_ref, load_sem)
     load.start()
@@ -116,6 +128,9 @@
     def block_at(index):
         return rows_at(index % 4 * BLOCK, BLOCK, BLOCK)
 
+    def half_of(rows, side):
+        return rows_at(rows.start + side * (BLOCK // 2), BLOCK // 2, BLOCK // 2)
+
     def fill(block, carry):
         chunk = (block % 4) * 4 + block // 4
         targets = (lax.broadcasted_iota(jnp.int32, (CHUNK, LANES), 0) + chunk * CHUNK + 1).astype(jnp.float32)
@@ -133,15 +148,24 @@
     lax.fori_loop(0, SKETCH // CHUNK, fill, 0)
     load.wait()
 
-    x_copies = []
+    fold_copies = []
     for q in range(4):
         rows = block_at(near + 1 + q)
         terms = jnp.dot(hot[rows, :], jac_ref[...], preferred_element_type=jnp.float32)
         for lane in range(4):
             part[lane, rows, :] = terms[:, lane * LANES : (lane + 1) * LANES]
         if q == 0:
-            pl.semaphore_wait(barrier, len(links))
-        x_copies.append([push(part.at[(x + s) % 4, rows, :], x_in.at[x, rows, :], "x", s) for s in (2, 1, 3)])
+            pl.semaphore_wait(barrier, len(beside))
+            vouch(0, [peer(me, "x", 3), peer(me, "y", 3), along_z(me, 1), along_z(me, -1)])
+        two_away = (x + 2) % 4
+        fold_copies.append(
+            [
+                push(part.at[two_away, half_of(rows, 0), :], fold_in.at[0, half_of(rows, 0), :], "x", 1),
+                push(part.at[two_away, half_of(rows, 1), :], fold_in.at[1, half_of(rows, 1), :], "x", 3),
+            ]
+        )
+    pl.semaphore_wait(known_sem.at[0], 4)
+    vouch(1, [along_z(me, 2), along_z(me, -2)])
 
     res_row = lax.dot_general(
         jnp.ones((RHS_ROWS, LANES), jnp.float32),
@@ -157,13 +181,25 @@
     )
     res_copies = [push(res_x.at[x], res_x.at[x], "x", s) for s in (1, 2, 3)]
 
+    x_copies = []
+    for q in range(4):
+        rows = block_at(near + 1 + q)
+        arrive(fold_copies[q])
+        for step, side in ((1, 0), (3, 1)):
+            index = (x + step) % 4
+            there = half_of(rows, side)
+            part[index, there, :] = part[index, there, :] + fold_in[side, there, :]
+        x_copies.append(
+            [push(part.at[(x + s) % 4, rows, :], x_in.at[side, rows, :], "x", s) for s, side in ((1, 0), (3, 1))]
+        )
+    pl.semaphore_wait(known_sem.at[1], 2)
+    vouch(2, [along_z(me, 4), along_z(me, -4)])
+
     near_copies = []
     for q in range(4):
         rows = block_at(near + 1 + q)
         arrive(x_copies[q])
-        summed = part[x, rows, :]
-        for s in (1, 2, 3):
-            summed = summed + x_in[(x + s) % 4, rows, :]
+        summed = part[x, rows, :] + x_in[0, rows, :] + x_in[1, rows, :]
         if q < 3:
             x_sum[rows, :] = summed
             near_copies.append(push(x_sum.at[rows, :], near_in.at[near], "near", q + 1))
@@ -176,6 +212,7 @@
     arrive(near_copies)
     near_sum[...] = near_in[0] + near_in[1] + near_in[2] + near_in[3]
 
+    pl.semaphore_wait(known_sem.at[2], 2)
     far_copies = []
     for s in (2, 1, 3):
         rows = rows_at((far + s) % 4 * CHUNK, CHUNK, CHUNK)
@@ -195,20 +232,28 @@
 
     far_copies = {s: push(own, own, "far", s) for s in (2, 1, 3)}
     near_copies = [push(own, own, "near", s) for s in (2, 1, 3)]
-    cols_copies = [push(own, own, "x", s) for s in (2, 1, 3)]
+    cols_copies = [[push(own, own, "x", s) for s in (1, 3)], [], [], []]
     arrive(res_copies)
     rhs_ref[...] = (res_far[0] + res_far[1] + res_far[2] + res_far[3]) * scaling
     for s in (1, 3, 2):
         arrive([far_copies[s]])
         chunk = chunk_of(near, far - s + 4)
         near_copies += [push(chunk, chunk, "near", t) for t in (2, 1, 3)]
-        cols_copies += [push(chunk, chunk, "x", t) for t in (2, 1, 3)]
+        cols_copies[0] += [push(chunk, chunk, "x", t) for t in (1, 3)]
     arrive(near_copies)
 
     def share(step):
         block = cols_ref.at[x, block_at(near + step), :]
-        cols_copies.extend([push(block, block, "x", t) for t in (2, 1, 3)])
-
+        cols_copies[step] += [push(block, block, "x", t) for t in (1, 3)]
+
+    def share_on(step):
+        arrive(cols_copies[step])
+        for t, side in ((1, 0), (3, 1)):
+            there = cols_ref.at[(x - t + 4) % 4, half_of(block_at(near + step), side), :]
+            on_copies.append(push(there, there, "x", t))
+
+    on_copies = []
+    share_on(0)
     share(1)
 
     values = cols_ref[x]
@@ -264,6 +309,7 @@
             [push(l_out.at[rows_at((index + s) % 4 * strip, strip), :], l_in.at[index], axis, s) for s in (2, 1, 3)]
         )
         l_in[index] = l_out[rows_at(index * strip, strip), :]
+    share_on(1)
     share(2)
     second_back = []
     for (first, count), copies, (_, axis, outer, inner, _, _, l_in) in zip(spans, second_copies, orders):
@@ -272,6 +318,7 @@
         piece = tri_ref.at[rows_at(half + first + outer * (count // 4) + inner * strip, strip), :]
         piece[...] = l_in[0] + l_in[1] + l_in[2] + l_in[3]
         second_back.append([push(piece, piece, axis, s) for s in (2, 1, 3)])
+    share_on(2)
     share(3)
 
     def quarter(first, count, index):
@@ -284,6 +331,7 @@
         piece = quarter(first, count, outer)
         first_back.append([push(piece, piece, axis, s) for s in (2, 1, 3)])
         last_copies.append(push(piece, piece, "core", 1))
+    share_on(3)
     for (first, count), copies, (_, _, outer, _, _, _, _) in zip(spans, first_back, orders):
         for s, copy in zip((2, 1, 3), copies):
             arrive([copy])
@@ -291,12 +339,12 @@
             last_copies.append(push(piece, piece, "core", 1))
     assert used[0] == COPIES
     arrive(last_copies)
-    arrive(cols_copies)
+    arrive(on_copies)
     for copy in sent:
         copy.wait_send()
 
 
-COPIES = 97
+COPIES = 102
 
 
 def gather(jacobian, coded, residual, scaling):
@@ -306,7 +354,8 @@
         ((SKETCH, DEV_ROWS), jnp.bfloat16),
         ((SKETCH, LANES), f32),
         ((4, SKETCH, LANES), f32),
-        ((4, SKETCH, LANES), f32),
+        ((2, SKETCH, LANES), f32),
+        ((2, SKETCH, LANES), f32),
         ((SKETCH, LANES), f32),
         ((4, BLOCK, LANES), f32),
         ((BLOCK, LANES), f32),
@@ -337,6 +386,7 @@
         out_specs=[pl.BlockSpec(memory_space=pltpu.VMEM)] * 3,
         scratch_shapes=[pltpu.VMEM(shape, kind) for shape, kind in shapes]
         + [
+            pltpu.SemaphoreType.REGULAR((3,)),
             pltpu.SemaphoreType.DMA,
             pltpu.SemaphoreType.DMA((COPIES,)),
             pltpu.SemaphoreType.DMA((COPIES,)),

time: 103 us -> 97.8 us (0.950)
  Pallas kernels: 101 us -> 96.3 us
    pallas_call x1, Pallas kernels: 90.9 us -> 86.1 us  [gather(): pl.pallas_call(functools.partial(gather_kernel, scaling), out_shape=(jax....]
where the time goes in v4:
time: 97.8 us; the launch traced here: 97.6 us
  Pallas kernels  96.3 us (98%)
    pallas_call x1, Pallas kernels, gather(): pl.pallas_call(functools.partial(gather_kernel, scaling), out_shape=(jax....  86.1 us
    pallas_call x1, Pallas kernels, solve(): pl.pallas_call(solve_kernel, out_shape=(jax.ShapeDtypeStruct((1, DEV_COLS...  10.2 us

profile of v4, /device:TPU:1, one launch (start us, length us, event | category | flops | bytes accessed | tf_op | source)
XLA Modules:
  0.0 97.6 jit_solution(1328855914829979914)
XLA Ops:
  0.6 0.7 multiply_bitcast_fusion
  1.4 86.1 %sketch_and_kernel.1 = (f32[2816,128]{1,0:T(8,128)S(1)}, f32[8,128]{1,0:T(8,128)S(1)}, f32[4,768,128]{2,1,0:T(8,128)S(1)}) custom-call(bf16[2048,512]{1,0:T(8,128)(2,1)} %jac_hbm.1, f32[16,128]{1,0:T(8,128)S(1)} %get-tuple-element.13.coded_ref, f32[16,128]{1,0:T(8,128)S(1)} %get-tuple-element.12.res_ref), custom_call_target="tpu_custom_call" | custom-call | tf_op jit(solution)/shard_map/sketch_and_kernel/pallas_call | solution.py:378
  87.5 10.2 %solve.1 = (f32[1,512]{1,0:T(1,128)}, f32[12,512]{1,0:T(8,128)}) custom-call(f32[2816,128]{1,0:T(8,128)S(1)} %get-tuple-element.7.tri_ref, f32[8,128]{1,0:T(8,128)S(1)} %get-tuple-element.8.rhs_ref, f32[4,768,128]{2,1,0:T(8,128)S(1)} %get-tuple-element.9.cols_ref), custom_call_target="tpu_custom_call" | custom-call | tf_op jit(solution)/shard_map/solve/pallas_call | solution.py:522

commit v5 on v4

--- a/solution.py
+++ b/solution.py
@@ -25,10 +25,11 @@
 RHS_ROWS = 8
 MESH = pl.DeviceIdType.MESH
 HIGHEST = lax.Precision.HIGHEST
-STOP_TOL = 3e-6
-ACCEPT_TOL = 1e-5
-ROUND_STEPS = 4
-MAX_ROUNDS = 16
+STOP_TOL = 1e-5
+ACCEPT_TOL = 2e-5
+FIRST_STEPS = 8
+ROUND_STEPS = 2
+MAX_ROUNDS = 30
 
 
 def place():
@@ -232,19 +233,16 @@
 
     far_copies = {s: push(own, own, "far", s) for s in (2, 1, 3)}
     near_copies = [push(own, own, "near", s) for s in (2, 1, 3)]
-    cols_copies = [[push(own, own, "x", s) for s in (1, 3)], [], [], []]
     arrive(res_copies)
     rhs_ref[...] = (res_far[0] + res_far[1] + res_far[2] + res_far[3]) * scaling
     for s in (1, 3, 2):
         arrive([far_copies[s]])
         chunk = chunk_of(near, far - s + 4)
         near_copies += [push(chunk, chunk, "near", t) for t in (2, 1, 3)]
-        cols_copies[0] += [push(chunk, chunk, "x", t) for t in (1, 3)]
-    arrive(near_copies)
 
     def share(step):
         block = cols_ref.at[x, block_at(near + step), :]
-        cols_copies[step] += [push(block, block, "x", t) for t in (1, 3)]
+        cols_copies.append([push(block, block, "x", t) for t in (1, 3)])
 
     def share_on(step):
         arrive(cols_copies[step])
@@ -252,8 +250,10 @@
             there = cols_ref.at[(x - t + 4) % 4, half_of(block_at(near + step), side), :]
             on_copies.append(push(there, there, "x", t))
 
+    cols_copies = []
     on_copies = []
-    share_on(0)
+    share(0)
+    arrive(near_copies)
     share(1)
 
     values = cols_ref[x]
@@ -278,6 +278,8 @@
             tri[base : base + LANES, :] = product[:, j * LANES : (j + 1) * LANES]
             base += LANES
     tri[base:, :] = jnp.zeros((TRI_ROWS - base, LANES), jnp.float32)
+
+    share_on(0)
 
     half = core * HALF
     other = (1 - core) * HALF
@@ -344,7 +346,7 @@
         copy.wait_send()
 
 
-COPIES = 102
+COPIES = 96
 
 
 def gather(jacobian, coded, residual, scaling):
@@ -451,28 +453,30 @@
         return (tol * tol * scale - 2.0 * total_of(res * res))[0, 0] >= 0.0
 
     def step(_, carry):
-        sol, res, way, size = carry
+        sol, res, way = carry
         image = product(way)
+        size = total_of(res * res)
         curve = total_of(way * image)
+        cross = total_of(res * image)
+        square = total_of(image * image)
         alpha = jnp.where(curve > 0, size / curve, 0.0)
-        sol = sol + alpha * way
+        new_size = jnp.maximum(size + alpha * (alpha * square - 2.0 * cross), 0.0)
+        beta = jnp.where(size > 0, new_size / size, 0.0)
         res = res - alpha * image
-        new_size = total_of(res * res)
-        beta = jnp.where(size > 0, new_size / size, 0.0)
-        return (sol, res, res + beta * way, new_size)
+        return (sol + alpha * way, res, res + beta * way)
 
     def round_of(carry):
         count, _, state = carry
-        state = lax.fori_loop(0, ROUND_STEPS, step, state)
+        state = lax.fori_loop(0, jnp.where(count == 0, FIRST_STEPS, ROUND_STEPS), step, state)
         return (count + 1, met(state[0], state[1], STOP_TOL), state)
 
     def go_on(carry):
         count, done, _ = carry
         return jnp.logical_and(count < MAX_ROUNDS, jnp.logical_not(done))
 
-    start = (jnp.zeros_like(rhs), rhs, rhs, total_of(rhs * rhs))
+    start = (jnp.zeros_like(rhs), rhs, rhs)
     first_done = largest[0, 0] <= 0.0
-    _, _, (sol, _, _, _) = lax.while_loop(go_on, round_of, (0, first_done, start))
+    _, _, (sol, _, _) = lax.while_loop(go_on, round_of, (0, first_done, start))
     true_res = rhs - product(sol)
     good = met(sol, true_res, ACCEPT_TOL)
     to_column(sol)

time: 97.8 us -> 96.1 us (0.983)
  Pallas kernels: 96.3 us -> 94.5 us
    pallas_call x1, Pallas kernels: 10.2 us -> 8.53 us  [solve(): pl.pallas_call(solve_kernel, out_shape=(jax.ShapeDtypeStruct((1, DEV_COLS...]
where the time goes in v5:
time: 96.1 us; the launch traced here: 95.9 us
  Pallas kernels  94.5 us (98%)
    pallas_call x1, Pallas kernels, gather(): pl.pallas_call(functools.partial(gather_kernel, scaling), out_shape=(jax....  86 us
    pallas_call x1, Pallas kernels, solve(): pl.pallas_call(solve_kernel, out_shape=(jax.ShapeDtypeStruct((1, DEV_COLS...  8.53 us

profile of v5, /device:TPU:1, one launch (start us, length us, event | category | flops | bytes accessed | tf_op | source)
XLA Modules:
  0.0 95.9 jit_solution(12959129381471006943)
XLA Ops:
  0.6 0.7 multiply_bitcast_fusion
  1.4 86.0 %sketch_and_kernel.1 = (f32[2816,128]{1,0:T(8,128)S(1)}, f32[8,128]{1,0:T(8,128)S(1)}, f32[4,768,128]{2,1,0:T(8,128)S(1)}) custom-call(bf16[2048,512]{1,0:T(8,128)(2,1)} %jac_hbm.1, f32[16,128]{1,0:T(8,128)S(1)} %get-tuple-element.13.coded_ref, f32[16,128]{1,0:T(8,128)S(1)} %get-tuple-element.12.res_ref), custom_call_target="tpu_custom_call" | custom-call | tf_op jit(solution)/shard_map/sketch_and_kernel/pallas_call | solution.py:380
  87.3 8.5 %solve.1 = (f32[1,512]{1,0:T(1,128)}, f32[12,512]{1,0:T(8,128)}) custom-call(f32[2816,128]{1,0:T(8,128)S(1)} %get-tuple-element.7.tri_ref, f32[8,128]{1,0:T(8,128)S(1)} %get-tuple-element.8.rhs_ref, f32[4,768,128]{2,1,0:T(8,128)S(1)} %get-tuple-element.9.cols_ref), custom_call_target="tpu_custom_call" | custom-call | tf_op jit(solution)/shard_map/solve/pallas_call | solution.py:526

commit v6 on v5

--- a/solution.py
+++ b/solution.py
@@ -123,6 +123,10 @@
         for copy in copies:
             copy.wait_recv()
 
+    def drain(keep):
+        while len(sent) > keep:
+            sent.pop(0).wait_send()
+
     def rows_at(first, count, unit=8):
         return pl.ds(pl.multiple_of(first, unit), count)
 
@@ -132,21 +136,18 @@
     def half_of(rows, side):
         return rows_at(rows.start + side * (BLOCK // 2), BLOCK // 2, BLOCK // 2)
 
-    def fill(block, carry):
-        chunk = (block % 4) * 4 + block // 4
-        targets = (lax.broadcasted_iota(jnp.int32, (CHUNK, LANES), 0) + chunk * CHUNK + 1).astype(jnp.float32)
-        first = pl.multiple_of(block * CHUNK, CHUNK)
-        total = jnp.zeros((CHUNK, LANES), jnp.float32)
-        for group in range(GROUPS):
-            code = coded_ref[group : group + 1, :]
-            hit = jnp.abs(code) == targets
-            total = total + jnp.where(hit, res_ref[group : group + 1, :], 0.0)
-            signed = jnp.where(hit, jnp.where(code > 0.0, 1.0, -1.0), 0.0)
-            hot[pl.ds(first, CHUNK), group * LANES : (group + 1) * LANES] = signed.astype(jnp.bfloat16)
-        acc[pl.ds(first, CHUNK), :] = total
-        return carry
-
-    lax.fori_loop(0, SKETCH // CHUNK, fill, 0)
+    acc[...] = jnp.zeros_like(acc)
+    offset = (lax.broadcasted_iota(jnp.int32, (CHUNK, LANES), 0) + 1).astype(jnp.float32)
+    for group in range(GROUPS):
+        code = coded_ref[group : group + 1, :]
+        target = jnp.abs(code) - offset
+        signs = jnp.broadcast_to(jnp.where(code > 0.0, 1.0, -1.0), (CHUNK, LANES))
+        terms = jnp.broadcast_to(res_ref[group : group + 1, :], (CHUNK, LANES))
+        for block in range(SKETCH // CHUNK):
+            rows = slice(block * CHUNK, (block + 1) * CHUNK)
+            hit = target == float(((block % 4) * 4 + block // 4) * CHUNK)
+            hot[rows, group * LANES : (group + 1) * LANES] = jnp.where(hit, signs, 0.0).astype(jnp.bfloat16)
+            acc[rows, :] = acc[rows, :] + jnp.where(hit, terms, 0.0)
     load.wait()
 
     fold_copies = []
@@ -219,6 +220,7 @@
         rows = rows_at((far + s) % 4 * CHUNK, CHUNK, CHUNK)
         far_copies.append(push(near_sum.at[rows, :], far_in.at[far], "far", s))
     far_in[far] = near_sum[rows_at(far * CHUNK, CHUNK, CHUNK), :]
+    drain(6)
     arrive(res_copies)
     res_far[far] = res_near[0] + res_near[1] + res_near[2] + res_near[3]
     res_copies = [push(res_far.at[far], res_far.at[far], "far", s) for s in (1, 2, 3)]
@@ -253,6 +255,7 @@
     cols_copies = []
     on_copies = []
     share(0)
+    drain(14)
     arrive(near_copies)
     share(1)
 
@@ -265,21 +268,22 @@
     rhs_t[:, 0:LANES] = high
     rhs_t[:, LANES : 2 * LANES] = low
     rhs_t[:, 2 * LANES :] = high
-    base = 0
-    for i in range(BLOCKS):
-        width = (i + 1) * LANES
+    for pair in range(BLOCKS // 2):
+        first, width = pair * 2 * LANES, (pair + 1) * 2 * LANES
         product = lax.dot_general(
-            lhs[i * LANES : width, :],
+            lhs[first:width, :],
             rhs_t[0:width, :],
             (((1,), (1,)), ((), ())),
             preferred_element_type=jnp.float32,
         )
-        for j in range(i + 1):
-            tri[base : base + LANES, :] = product[:, j * LANES : (j + 1) * LANES]
-            base += LANES
+        for i in (2 * pair, 2 * pair + 1):
+            for j in range(i + 1):
+                base = (i * (i + 1) // 2 + j) * LANES
+                tri[base : base + LANES, :] = product[
+                    i * LANES - first : (i + 1) * LANES - first, j * LANES : (j + 1) * LANES
+                ]
+    base = BLOCKS * (BLOCKS + 1) // 2 * LANES
     tri[base:, :] = jnp.zeros((TRI_ROWS - base, LANES), jnp.float32)
-
-    share_on(0)
 
     half = core * HALF
     other = (1 - core) * HALF
@@ -288,6 +292,7 @@
         push(tri.at[rows_at(other + first, count), :], core_in.at[first : first + count, :], "core", 1)
         for first, count in spans
     ]
+    share_on(0)
     orders = (("x", "y", x, y, k_in_a, l_out_a, l_in_a), ("y", "x", y, x, k_in_b, l_out_b, l_in_b))
 
     first_copies = []
@@ -313,6 +318,7 @@
         l_in[index] = l_out[rows_at(index * strip, strip), :]
     share_on(1)
     share(2)
+    drain(12)
     second_back = []
     for (first, count), copies, (_, axis, outer, inner, _, _, l_in) in zip(spans, second_copies, orders):
         strip = count // 16
@@ -334,6 +340,7 @@
         first_back.append([push(piece, piece, axis, s) for s in (2, 1, 3)])
         last_copies.append(push(piece, piece, "core", 1))
     share_on(3)
+    drain(18)
     for (first, count), copies, (_, _, outer, _, _, _, _) in zip(spans, first_back, orders):
         for s, copy in zip((2, 1, 3), copies):
             arrive([copy])
@@ -342,8 +349,7 @@
     assert used[0] == COPIES
     arrive(last_copies)
     arrive(on_copies)
-    for copy in sent:
-        copy.wait_send()
+    drain(0)
 
 
 COPIES = 96

time: 96.1 us -> 94.6 us (0.984)
  Pallas kernels: 94.5 us -> 93 us
where the time goes in v6:
time: 94.6 us; the launch traced here: 94.4 us
  Pallas kernels  93 us (98%)
    pallas_call x1, Pallas kernels, gather(): pl.pallas_call(functools.partial(gather_kernel, scaling), out_shape=(jax....  85.4 us
    pallas_call x1, Pallas kernels, solve(): pl.pallas_call(solve_kernel, out_shape=(jax.ShapeDtypeStruct((1, DEV_COLS...  7.6 us

profile of v6, /device:TPU:1, one launch (start us, length us, event | category | flops | bytes accessed | tf_op | source)
XLA Modules:
  0.0 94.4 jit_solution(16372890874189525086)
XLA Ops:
  0.6 0.7 multiply_bitcast_fusion
  1.4 85.4 %sketch_and_kernel.1 = (f32[2816,128]{1,0:T(8,128)S(1)}, f32[8,128]{1,0:T(8,128)S(1)}, f32[4,768,128]{2,1,0:T(8,128)S(1)}) custom-call(bf16[2048,512]{1,0:T(8,128)(2,1)} %jac_hbm.1, f32[16,128]{1,0:T(8,128)S(1)} %get-tuple-element.13.coded_ref, f32[16,128]{1,0:T(8,128)S(1)} %get-tuple-element.12.res_ref), custom_call_target="tpu_custom_call" | custom-call | tf_op jit(solution)/shard_map/sketch_and_kernel/pallas_call | solution.py:386
  86.8 7.6 %solve.1 = (f32[1,512]{1,0:T(1,128)}, f32[12,512]{1,0:T(8,128)}) custom-call(f32[2816,128]{1,0:T(8,128)S(1)} %get-tuple-element.7.tri_ref, f32[8,128]{1,0:T(8,128)S(1)} %get-tuple-element.8.rhs_ref, f32[4,768,128]{2,1,0:T(8,128)S(1)} %get-tuple-element.9.cols_ref), custom_call_target="tpu_custom_call" | custom-call | tf_op jit(solution)/shard_map/solve/pallas_call | solution.py:532

commit v7 on v6

--- a/solution.py
+++ b/solution.py
@@ -27,7 +27,7 @@
 HIGHEST = lax.Precision.HIGHEST
 STOP_TOL = 1e-5
 ACCEPT_TOL = 2e-5
-FIRST_STEPS = 8
+FIRST_STEPS = 10
 ROUND_STEPS = 2
 MAX_ROUNDS = 30
 
@@ -292,7 +292,6 @@
         push(tri.at[rows_at(other + first, count), :], core_in.at[first : first + count, :], "core", 1)
         for first, count in spans
     ]
-    share_on(0)
     orders = (("x", "y", x, y, k_in_a, l_out_a, l_in_a), ("y", "x", y, x, k_in_b, l_out_b, l_in_b))
 
     first_copies = []
@@ -307,6 +306,8 @@
             ]
         )
         k_in[index] = k_out[rows_at(first + index * strip, strip), :]
+    share_on(0)
+    share(2)
     second_copies = []
     for (first, count), copies, (_, axis, _, index, k_in, l_out, l_in) in zip(spans, first_copies, orders):
         strip = count // 16
@@ -317,7 +318,7 @@
         )
         l_in[index] = l_out[rows_at(index * strip, strip), :]
     share_on(1)
-    share(2)
+    share(3)
     drain(12)
     second_back = []
     for (first, count), copies, (_, axis, outer, inner, _, _, l_in) in zip(spans, second_copies, orders):
@@ -327,7 +328,6 @@
         piece[...] = l_in[0] + l_in[1] + l_in[2] + l_in[3]
         second_back.append([push(piece, piece, axis, s) for s in (2, 1, 3)])
     share_on(2)
-    share(3)
 
     def quarter(first, count, index):
         return tri_ref.at[rows_at(half + first + index % 4 * (count // 4), count // 4), :]
@@ -485,7 +485,6 @@
     _, _, (sol, _, _) = lax.while_loop(go_on, round_of, (0, first_done, start))
     true_res = rhs - product(sol)
     good = met(sol, true_res, ACCEPT_TOL)
-    to_column(sol)
     answer[...] = column[...]
 
     @pl.when(jnp.logical_not(good))

time: 94.6 us -> 92.3 us (0.976)
  Pallas kernels: 93 us -> 90.8 us
    pallas_call x1, Pallas kernels: 85.4 us -> 83.3 us  [gather(): pl.pallas_call(functools.partial(gather_kernel, scaling), out_shape=(jax....]
where the time goes in v7:
time: 92.3 us; the launch traced here: 92.1 us
  Pallas kernels  90.8 us (98%)
    pallas_call x1, Pallas kernels, gather(): pl.pallas_call(functools.partial(gather_kernel, scaling), out_shape=(jax....  83.3 us
    pallas_call x1, Pallas kernels, solve(): pl.pallas_call(solve_kernel, out_shape=(jax.ShapeDtypeStruct((1, DEV_COLS...  7.43 us

profile of v7, /device:TPU:1, one launch (start us, length us, event | category | flops | bytes accessed | tf_op | source)
XLA Modules:
  0.0 92.1 jit_solution(5566602261650512871)
XLA Ops:
  0.6 0.7 multiply_bitcast_fusion
  1.4 83.3 %sketch_and_kernel.1 = (f32[2816,128]{1,0:T(8,128)S(1)}, f32[8,128]{1,0:T(8,128)S(1)}, f32[4,768,128]{2,1,0:T(8,128)S(1)}) custom-call(bf16[2048,512]{1,0:T(8,128)(2,1)} %jac_hbm.1, f32[16,128]{1,0:T(8,128)S(1)} %get-tuple-element.13.coded_ref, f32[16,128]{1,0:T(8,128)S(1)} %get-tuple-element.12.res_ref), custom_call_target="tpu_custom_call" | custom-call | tf_op jit(solution)/shard_map/sketch_and_kernel/pallas_call | solution.py:386
  84.7 7.4 %solve.1 = (f32[1,512]{1,0:T(1,128)}, f32[12,512]{1,0:T(8,128)}) custom-call(f32[2816,128]{1,0:T(8,128)S(1)} %get-tuple-element.7.tri_ref, f32[8,128]{1,0:T(8,128)S(1)} %get-tuple-element.8.rhs_ref, f32[4,768,128]{2,1,0:T(8,128)S(1)} %get-tuple-element.9.cols_ref), custom_call_target="tpu_custom_call" | custom-call | tf_op jit(solution)/shard_map/solve/pallas_call | solution.py:531

commit v8 on v7

--- a/solution.py
+++ b/solution.py
@@ -308,6 +308,7 @@
         k_in[index] = k_out[rows_at(first + index * strip, strip), :]
     share_on(0)
     share(2)
+    share(3)
     second_copies = []
     for (first, count), copies, (_, axis, _, index, k_in, l_out, l_in) in zip(spans, first_copies, orders):
         strip = count // 16
@@ -318,7 +319,6 @@
         )
         l_in[index] = l_out[rows_at(index * strip, strip), :]
     share_on(1)
-    share(3)
     drain(12)
     second_back = []
     for (first, count), copies, (_, axis, outer, inner, _, _, l_in) in zip(spans, second_copies, orders):
@@ -328,6 +328,7 @@
         piece[...] = l_in[0] + l_in[1] + l_in[2] + l_in[3]
         second_back.append([push(piece, piece, axis, s) for s in (2, 1, 3)])
     share_on(2)
+    share_on(3)
 
     def quarter(first, count, index):
         return tri_ref.at[rows_at(half + first + index % 4 * (count // 4), count // 4), :]
@@ -339,7 +340,6 @@
         piece = quarter(first, count, outer)
         first_back.append([push(piece, piece, axis, s) for s in (2, 1, 3)])
         last_copies.append(push(piece, piece, "core", 1))
-    share_on(3)
     drain(18)
     for (first, count), copies, (_, _, outer, _, _, _, _) in zip(spans, first_back, orders):
         for s, copy in zip((2, 1, 3), copies):

time: 92.3 us -> 94.4 us (1.023)
  Pallas kernels: 90.8 us -> 93.3 us
    pallas_call x1, Pallas kernels: 83.3 us -> 85 us  [gather(): pl.pallas_call(functools.partial(gather_kernel, scaling), out_shape=(jax....]
where the time goes in v8:
time: 94.4 us; the launch traced here: 94.7 us
  Pallas kernels  93.3 us (99%)
    pallas_call x1, Pallas kernels, gather(): pl.pallas_call(functools.partial(gather_kernel, scaling), out_shape=(jax....  85 us
    pallas_call x1, Pallas kernels, solve(): pl.pallas_call(solve_kernel, out_shape=(jax.ShapeDtypeStruct((1, DEV_COLS...  8.36 us

profile of v8, /device:TPU:1, one launch (start us, length us, event | category | flops | bytes accessed | tf_op | source)
XLA Modules:
  0.0 94.7 jit_solution(13600846491292205454)
XLA Ops:
  0.6 0.7 multiply_bitcast_fusion
  1.4 85.0 %sketch_and_kernel.1 = (f32[2816,128]{1,0:T(8,128)S(1)}, f32[8,128]{1,0:T(8,128)S(1)}, f32[4,768,128]{2,1,0:T(8,128)S(1)}) custom-call(bf16[2048,512]{1,0:T(8,128)(2,1)} %jac_hbm.1, f32[16,128]{1,0:T(8,128)S(1)} %get-tuple-element.13.coded_ref, f32[16,128]{1,0:T(8,128)S(1)} %get-tuple-element.12.res_ref), custom_call_target="tpu_custom_call" | custom-call | tf_op jit(solution)/shard_map/sketch_and_kernel/pallas_call | solution.py:386
  86.3 8.4 %solve.1 = (f32[1,512]{1,0:T(1,128)}, f32[12,512]{1,0:T(8,128)}) custom-call(f32[2816,128]{1,0:T(8,128)S(1)} %get-tuple-element.7.tri_ref, f32[8,128]{1,0:T(8,128)S(1)} %get-tuple-element.8.rhs_ref, f32[4,768,128]{2,1,0:T(8,128)S(1)} %get-tuple-element.9.cols_ref), custom_call_target="tpu_custom_call" | custom-call | tf_op jit(solution)/shard_map/solve/pallas_call | solution.py:531
